TPU v7x, 32 devices: a whole 2x2x4 slice. The times are simulated.
32 devices in a mesh: band: 16 (over z, x, core), slab: 2 (over y).
Axes of the slice: x: 2, y: 2, z: 4, core: 2. Of those that a mesh axis runs over, the one named last changes fastest.
Arguments:
- orbitals: float32 [64, 96, 4608], P('band', 'slab'), may hold values from -3 to 3
- owner: int32 [2], replicated, may hold values from 0 to 15
- picks: int32 [2, 2], replicated, may hold values from 0 to 3
Outputs:
- exchange_field: float32 [64, 96, 4608], P('band', 'slab')
- transposed: float32 [2, 2, 96, 4608], P(None, None, 'slab')
Inputs may be any that keep to these rules, and one draw needn't show every extreme that they name: owner names a band group and picks positions within it; the two picks of a step may coincide.
All inputs are finite; a program needn't handle non-finite values.
Results may differ from a plain program's by a relative error of at most 0.0001.
Values sent between devices are 32-bit elements; how exact they have to be, the bound alone decides.
A program may use at most 128 MiB of HBM per device.

v0:
```python
import math

import jax
import jax.numpy as jnp
from jax import lax
from jax.sharding import PartitionSpec as P

NX = 48
NY = 96
NZ = 96
STEPS = 2


length_first = 41.05
length_side = 41.05
length_last = 20.525
omega_screen = 0.106


def broadcast(x, axis, root):
    mine = lax.axis_index(axis) == root
    return lax.psum(jnp.where(mine, x, jnp.zeros_like(x)), axis)


def frequency(counter, length):
    return jnp.where(counter <= length // 2, counter, counter - length).astype(jnp.float32)


def coulomb_kernel(freq_z, freq_y, freq_x):
    wave_first = 2.0 * math.pi / length_first
    wave_side = 2.0 * math.pi / length_side
    wave_last = 2.0 * math.pi / length_last
    squared = (
        (wave_first * freq_z)[:, None, None] ** 2
        + (wave_side * freq_y)[None, :, None] ** 2
        + (wave_last * freq_x)[None, None, :] ** 2
    )
    safe = jnp.where(squared > 0, squared, 1.0)
    screened = -4.0 * math.pi * jnp.expm1(-squared / (4.0 * omega_screen**2)) / safe
    return jnp.where(squared > 0, screened, math.pi / omega_screen**2)


def dft_table(length, direction):
    counter = jnp.arange(length)
    product = counter[:, None] * counter[None, :] % length
    angle = 2.0 * math.pi / length * product.astype(jnp.float32)
    return (jnp.cos(angle), direction * jnp.sin(angle))


def along_last(values, length, direction):
    cosines, sine_table = dft_table(length, direction)
    upper = jnp.concatenate([cosines, -sine_table], axis=1)
    lower = jnp.concatenate([sine_table, cosines], axis=1)
    matrix = jnp.concatenate([upper, lower], axis=0)
    return jnp.matmul(values, matrix, precision=lax.Precision.HIGHEST)


def along_axis(values, length, direction, pattern):
    cosines, sine_table = dft_table(length, direction)
    middle = values.shape[-1] // 2
    with_cos = jnp.einsum(pattern, cosines, values, precision=lax.Precision.HIGHEST)
    with_sin = jnp.einsum(pattern, sine_table, values, precision=lax.Precision.HIGHEST)
    real_part = with_cos[..., :middle] + with_sin[..., middle:]
    imag_part = with_cos[..., middle:] - with_sin[..., :middle]
    return jnp.concatenate([real_part, imag_part], axis=-1)


def per_device(orbitals, owner, picks):
    bloc, planes, points = orbitals.shape
    slab_count = lax.axis_size("slab")
    column_rows = NY // slab_count
    slab_index = lax.axis_index("slab")
    freq_y = frequency(slab_index * column_rows + jnp.arange(column_rows), NY)
    kernel = coulomb_kernel(frequency(jnp.arange(NZ), NZ), freq_y, frequency(jnp.arange(NX), NX))
    kernel = kernel * (1.0 / (NX * NY * NZ))
    kernel_tile = jnp.concatenate([kernel, kernel], axis=-1)
    exchange_sum = jnp.zeros_like(orbitals)
    collected = []
    for turn_index in range(STEPS):
        fetch_chosen = jnp.take(orbitals, picks[turn_index], axis=0)
        chosen = broadcast(fetch_chosen, "band", owner[turn_index])
        real_part = (orbitals * chosen[0]).reshape(bloc, planes, NY, NX)
        imag_part = (orbitals * chosen[1]).reshape(bloc, planes, NY, NX)
        fields = jnp.concatenate([real_part, imag_part], axis=-1)
        fields = along_last(fields, NX, 1.0)
        fields = along_axis(fields, NY, 1.0, "ky,bzyx->bzkx")
        columns = lax.all_to_all(fields, "slab", split_axis=2, concat_axis=1, tiled=True)
        columns = along_axis(columns, NZ, 1.0, "kz,bzyx->bkyx") * kernel_tile
        columns = along_axis(columns, NZ, -1.0, "kz,bzyx->bkyx")
        fields = lax.all_to_all(columns, "slab", split_axis=1, concat_axis=2, tiled=True)
        fields = along_axis(fields, NY, -1.0, "ky,bzyx->bzkx")
        fields = along_last(fields, NX, -1.0)
        count = fields.shape[0]
        potentials_first_part = fields[..., :NX].reshape(count, planes, points)
        potentials_second_part = fields[..., NX:].reshape(count, planes, points)
        applied = potentials_first_part * chosen[0] + potentials_second_part * chosen[1]
        contributions_local_sum = jnp.stack(
            [
                jnp.sum(potentials_first_part * orbitals, axis=0),
                jnp.sum(potentials_second_part * orbitals, axis=0),
            ]
        )
        applied, local_sum = (applied, contributions_local_sum)
        exchange_sum = exchange_sum + applied
        collected.append(lax.psum(local_sum, "band"))
    transposed = jnp.stack(collected)
    return (exchange_sum, transposed)


def solution(mesh):
    in_specs = (P("band", "slab", None), P(), P())
    out_specs = (P("band", "slab", None), P(None, None, "slab", None))
    return jax.shard_map(
        per_device, mesh=mesh, in_specs=in_specs, out_specs=out_specs, check_vma=False
    )
```

profile of v0, /device:TPU:0, one launch (start us, length us, event | category | flops | bytes accessed | tf_op | source)
XLA Modules:
  0.0 941.9 jit_solution(16595242339337165579)
XLA Ops:
  22.3 107.6 %all-reduce.7.cloned.1.call-done = (f32[2,48,4608]{2,1,0:T(8,128)}, f32[2,48,4608]{2,1,0:T(8,128)}) async-done(((f32[2,48,4608]{2,1,0:T(8,128)}, f32[2,48,4608]{2,1,0:T(8,128)}), (f32[2,48,4608]{2,1,0:T(8,128)}, f32[2,48,4608]{2,1,0:T(8,128)})) %all-reduce.7.cloned.1.call-update) | async-done | bytes 3538960 | tf_op jit(solution)/shard_map/psum | solution.py:22
  137.9 8.5 reshape.105
  152.6 26.6 %fusion.8 = f32[4,48,96,96]{2,3,1,0:T(8,128)S(1)} fusion(f32[4,48,96,48]{3,2,1,0:T(8,128)} %reshape.106, f32[4,48,96,48]{3,2,1,0:T(8,128)} %reshape.105, f32[48,48]{1,0:T(8,128)} %get-tuple-element.51, f32[48,48]{1,0:T(8,128)} %get-tuple-element.50, f32[48,48]{1,0:T(8,128)} %fusion.141), kind=kOutput, calls=%fused_computation.13 | convolution fusion | flops 2040228864 | bytes 14183424 | tf_op jit(solution)/shard_map/dot_general | solution.py:55
  179.3 8.9 convolution_bitcast_fusion.4
  188.2 10.5 %convolution_bitcast_fusion.5 = f32[4,48,96,96]{2,3,1,0:T(8,128)} fusion(f32[4,48,96,96]{2,3,1,0:T(8,128)S(1)} %fusion.8), kind=kOutput, calls=%fused_computation.63 | convolution fusion | flops 2038514688 | bytes 14155776 | tf_op jit(solution)/shard_map/ky,bzyx->bzkx/dot_general | solution.py:61
  211.9 11.4 %copy.63 = f32[4,48,96,96]{3,1,0,2:T(8,128)} copy(f32[4,48,96,96]{2,3,1,0:T(8,128)} %pad_maximum_fusion.2) | data formatting | bytes 14155776 | tf_op jit(solution)/shard_map/concatenate | solution.py:65
  231.8 8.7 reshape.101
  240.5 8.3 reshape.102
  248.8 25.0 %fusion = f32[4,48,96,96]{2,3,1,0:T(8,128)S(1)} fusion(f32[4,48,96,48]{3,2,1,0:T(8,128)} %reshape.102, f32[4,48,96,48]{3,2,1,0:T(8,128)} %reshape.101, f32[48,48]{1,0:T(8,128)S(1)} %copy-done.10, f32[48,48]{1,0:T(8,128)S(1)} %copy-done.13, f32[48,48]{1,0:T(8,128)S(1)} %copy-done.12), kind=kOutput, calls=%fused_computation.2 | convolution fusion | flops 2040228864 | bytes 14183424 | tf_op jit(solution)/shard_map/dot_general | solution.py:55
  273.8 8.9 convolution_bitcast_fusion.10
  282.8 10.6 %convolution_bitcast_fusion.11 = f32[4,48,96,96]{2,3,1,0:T(8,128)} fusion(f32[4,48,96,96]{2,3,1,0:T(8,128)S(1)} %fusion), kind=kOutput, calls=%fused_computation.69 | convolution fusion | flops 2038514688 | bytes 14155776 | tf_op jit(solution)/shard_map/ky,bzyx->bzkx/dot_general | solution.py:61
  300.2 8.6 pad_maximum_fusion
  308.7 11.4 %copy.47 = f32[4,48,96,96]{3,1,0,2:T(8,128)} copy(f32[4,48,96,96]{2,3,1,0:T(8,128)} %pad_maximum_fusion) | data formatting | bytes 14155776 | tf_op jit(solution)/shard_map/concatenate | solution.py:65
  320.1 13.2 %all-to-all-done.2 = f32[4,48,96,96]{3,1,0,2:T(8,128)} async-done(((f32[4,48,96,96]{3,1,0,2:T(8,128)}), f32[4,48,96,96]{3,1,0,2:T(8,128)}, u32[]{:S(2)}, u32[]{:S(2)}) %all-to-all-start.2) | async-done | bytes 7077920 | tf_op jit(solution)/shard_map/all_to_all | solution.py:87
  340.6 12.7 %copy.65 = f32[4,2,48,48,96]{4,3,2,1,0:T(8,128)} copy(f32[4,2,48,48,96]{4,2,0,3,1:T(8,128)} %bitcast.41) | data formatting | bytes 14155776 | tf_op jit(solution)/shard_map/all_to_all | solution.py:87
  353.2 10.3 %copy.66 = f32[4,96,48,96]{1,3,2,0:T(8,128)} copy(f32[4,96,48,96]{3,2,1,0:T(8,128)} %bitcast.152) | data formatting | bytes 14155776 | tf_op jit(solution)/shard_map/all_to_all | solution.py:87
  363.5 11.1 %convolution_bitcast_fusion.2 = f32[4,96,48,96]{1,3,2,0:T(8,128)S(1)} fusion(f32[4,96,48,96]{1,3,2,0:T(8,128)} %copy.66), kind=kOutput, calls=%fused_computation.60 | convolution fusion | flops 2038514688 | bytes 14155776 | tf_op jit(solution)/shard_map/kz,bzyx->bkyx/dot_general | solution.py:62
  374.7 10.3 %convolution_bitcast_fusion.3 = f32[4,96,48,96]{1,3,2,0:T(8,128)} fusion(f32[4,96,48,96]{1,3,2,0:T(8,128)S(1)} %copy-done), kind=kOutput, calls=%fused_computation.61 | convolution fusion | flops 2038514688 | bytes 14155776 | tf_op jit(solution)/shard_map/kz,bzyx->bkyx/dot_general | solution.py:61
  390.0 8.6 fusion.26
  398.6 11.9 %fusion.27 = f32[4,96,48,96]{1,3,2,0:T(8,128)} fusion(f32[4,96,48,48]{1,3,2,0:T(8,128)S(1)} %get-tuple-element.28, f32[4,96,48,48]{1,3,2,0:T(8,128)S(1)} %get-tuple-element.27, f32[96,48,96]{0,2,1:T(8,128)S(1)} %pad_maximum_fusion.5), kind=kOutput, calls=%fused_computation.57 | convolution fusion | flops 2042062848 | bytes 15925248 | tf_op jit(solution)/shard_map/kz,bzyx->bkyx/dot_general | solution.py:62
  423.7 11.4 %copy.68 = f32[4,96,48,96]{3,2,0,1:T(8,128)} copy(f32[4,96,48,96]{1,3,2,0:T(8,128)} %pad_maximum_fusion.3) | data formatting | bytes 14155776 | tf_op jit(solution)/shard_map/concatenate | solution.py:65
  442.2 7.6 all-to-all-start.3
  449.8 12.7 %copy.49 = f32[4,2,48,48,96]{4,3,2,1,0:T(8,128)} copy(f32[4,2,48,48,96]{4,2,0,3,1:T(8,128)} %bitcast.14) | data formatting | bytes 14155776 | tf_op jit(solution)/shard_map/all_to_all | solution.py:87
  462.5 10.3 %copy.50 = f32[4,96,48,96]{1,3,2,0:T(8,128)} copy(f32[4,96,48,96]{3,2,1,0:T(8,128)} %bitcast.153) | data formatting | bytes 14155776 | tf_op jit(solution)/shard_map/all_to_all | solution.py:87
  472.8 11.1 %convolution_bitcast_fusion.8 = f32[4,96,48,96]{1,3,2,0:T(8,128)S(1)} fusion(f32[4,96,48,96]{1,3,2,0:T(8,128)} %copy.50), kind=kOutput, calls=%fused_computation.66 | convolution fusion | flops 2038514688 | bytes 14155776 | tf_op jit(solution)/shard_map/kz,bzyx->bkyx/dot_general | solution.py:62
  484.0 10.4 %convolution_bitcast_fusion.9 = f32[4,96,48,96]{1,3,2,0:T(8,128)} fusion(f32[4,96,48,96]{1,3,2,0:T(8,128)S(1)} %copy-done.1), kind=kOutput, calls=%fused_computation.67 | convolution fusion | flops 2038514688 | bytes 14155776 | tf_op jit(solution)/shard_map/kz,bzyx->bkyx/dot_general | solution.py:61
  499.5 8.6 fusion.24
  508.1 11.9 %fusion.25 = f32[4,96,48,96]{1,3,2,0:T(8,128)} fusion(f32[4,96,48,48]{1,3,2,0:T(8,128)S(1)} %get-tuple-element.20, f32[4,96,48,48]{1,3,2,0:T(8,128)S(1)} %get-tuple-element.19, f32[96,48,96]{0,2,1:T(8,128)S(1)} %pad_maximum_fusion.5), kind=kOutput, calls=%fused_computation.55 | convolution fusion | flops 2042062848 | bytes 15925248 | tf_op jit(solution)/shard_map/kz,bzyx->bkyx/dot_general | solution.py:62
  529.5 11.4 %copy.52 = f32[4,96,48,96]{3,2,0,1:T(8,128)} copy(f32[4,96,48,96]{1,3,2,0:T(8,128)} %pad_maximum_fusion.1) | data formatting | bytes 14155776 | tf_op jit(solution)/shard_map/concatenate | solution.py:65
  540.9 9.7 %all-to-all-done.3 = f32[4,96,48,96]{3,2,0,1:T(8,128)} async-done(((f32[4,96,48,96]{3,2,0,1:T(8,128)}), f32[4,96,48,96]{3,2,0,1:T(8,128)}, u32[]{:S(2)}, u32[]{:S(2)}) %all-to-all-start.3) | async-done | bytes 7077920 | tf_op jit(solution)/shard_map/all_to_all | solution.py:90
  563.2 18.1 %convolution_bitcast_fusion = f32[4,48,96,96]{2,3,1,0:T(8,128)} fusion(f32[4,48,96,96]{3,2,1,0:T(8,128)S(1)} %bitcast.144), kind=kOutput, calls=%fused_computation.58 | convolution fusion | flops 2038523904 | bytes 14155776 | tf_op jit(solution)/shard_map/ky,bzyx->bzkx/dot_general | solution.py:62
  581.3 18.2 %convolution_bitcast_fusion.1 = f32[4,48,96,96]{2,3,1,0:T(8,128)} fusion(f32[4,48,96,96]{3,2,1,0:T(8,128)S(1)} %bitcast.145), kind=kOutput, calls=%fused_computation.59 | convolution fusion | flops 2038514688 | bytes 14155776 | tf_op jit(solution)/shard_map/ky,bzyx->bzkx/dot_general | solution.py:61
  599.5 58.2 %all-to-all-done.1 = f32[4,96,48,96]{3,2,0,1:T(8,128)} async-done(((f32[4,96,48,96]{3,2,0,1:T(8,128)}), f32[4,96,48,96]{3,2,0,1:T(8,128)}, u32[]{:S(2)}, u32[]{:S(2)}) %all-to-all-start.1) | async-done | bytes 7077920 | tf_op jit(solution)/shard_map/all_to_all | solution.py:90
  662.9 18.3 %convolution_bitcast_fusion.6 = f32[4,48,96,96]{2,3,1,0:T(8,128)} fusion(f32[4,48,96,96]{3,2,1,0:T(8,128)S(1)} %bitcast.146), kind=kOutput, calls=%fused_computation.64 | convolution fusion | flops 2038523904 | bytes 14155776 | tf_op jit(solution)/shard_map/ky,bzyx->bzkx/dot_general | solution.py:62
  681.2 18.2 %convolution_bitcast_fusion.7 = f32[4,48,96,96]{2,3,1,0:T(8,128)} fusion(f32[4,48,96,96]{3,2,1,0:T(8,128)S(1)} %bitcast.147), kind=kOutput, calls=%fused_computation.65 | convolution fusion | flops 2038514688 | bytes 14155776 | tf_op jit(solution)/shard_map/ky,bzyx->bzkx/dot_general | solution.py:61
  704.2 11.7 %fusion.12 = f32[4,48,96,96]{2,3,1,0:T(8,128)S(1)} fusion(f32[4,48,96,48]{2,3,1,0:T(8,128)} %get-tuple-element.24, f32[4,48,96,48]{2,3,1,0:T(8,128)} %get-tuple-element.23, f32[48,48]{1,0:T(8,128)S(1)} %copy-done.11, f32[48,48]{1,0:T(8,128)S(1)} %get-tuple-element.52, f32[48,48]{1,0:T(8,128)S(1)} %get-tuple-element.53), kind=kOutput, calls=%fused_computation.20 | convolution fusion | flops 2040228864 | bytes 14183424 | tf_op jit(solution)/shard_map/dot_general | solution.py:55
  720.5 7.9 copy.75
  728.4 10.2 %reshape.107 = f32[4,48,4608]{2,1,0:T(8,128)} reshape(f32[4,48,96,48]{3,2,1,0:T(8,128)} %copy.75) | data formatting | bytes 7077888 | tf_op jit(solution)/shard_map/reshape | solution.py:94
  738.6 7.9 copy.76
  746.5 10.3 %reshape.108 = f32[4,48,4608]{2,1,0:T(8,128)} reshape(f32[4,48,96,48]{3,2,1,0:T(8,128)} %copy.76) | data formatting | bytes 7077888 | tf_op jit(solution)/shard_map/reshape | solution.py:95
  756.8 7.4 slice_add_fusion.4
  764.1 9.8 %fusion.4 = f32[4,48,96,96]{2,3,1,0:T(8,128)S(1)} fusion(f32[4,48,96,48]{2,3,1,0:T(8,128)S(1)} %get-tuple-element.16, f32[4,48,96,48]{2,3,1,0:T(8,128)S(1)} %get-tuple-element.15, f32[48,48]{1,0:T(8,128)S(1)} %copy-done.11, f32[48,48]{1,0:T(8,128)S(1)} %get-tuple-element.52, f32[48,48]{1,0:T(8,128)S(1)} %get-tuple-element.53), kind=kOutput, calls=%fused_computation.9 | convolution fusion | flops 2040228864 | bytes 14183424 | tf_op jit(solution)/shard_map/dot_general | solution.py:55
  778.4 7.9 copy.59
  786.2 10.2 %reshape.103 = f32[4,48,4608]{2,1,0:T(8,128)} reshape(f32[4,48,96,48]{3,2,1,0:T(8,128)} %copy.59) | data formatting | bytes 7077888 | tf_op jit(solution)/shard_map/reshape | solution.py:94
  796.4 7.9 copy.60
  804.3 10.6 %reshape.104 = f32[4,48,4608]{2,1,0:T(8,128)} reshape(f32[4,48,96,48]{3,2,1,0:T(8,128)} %copy.60) | data formatting | bytes 7077888 | tf_op jit(solution)/shard_map/reshape | solution.py:95
  814.9 9.3 multiply_reduce_fusion.3
  827.0 103.5 %all-reduce.5.cloned.1.call-done = (f32[1,2,48,4608]{3,2,1,0:T(8,128)}, f32[1,2,48,4608]{3,2,1,0:T(8,128)}) async-done(((f32[1,2,48,4608]{3,2,1,0:T(8,128)}, f32[1,2,48,4608]{3,2,1,0:T(8,128)}), (f32[1,2,48,4608]{3,2,1,0:T(8,128)}, f32[1,2,48,4608]{3,2,1,0:T(8,128)})) %all-reduce.5.cloned.1.call-update) | async-done | bytes 3538960 | tf_op jit(solution)/shard_map/psum | solution.py:105
  (87 shorter events, 142.0 us)
Async XLA Ops:
  7.2 5.0 copy-start.2
  7.2 122.7 %all-reduce.7.cloned.1.call-start = ((), (), s32[]{:S(2)}) async-start(), calls=%async_computation.5 | async-start | bytes 7077888 | tf_op jit(solution)/shard_map/psum | solution.py:22
  129.9 2.0 copy-start.9
  131.6 6.3 copy-start.5
  131.6 6.3 copy-start.6
  132.0 5.9 copy-start.7
  132.0 5.9 copy-start.8
  137.9 8.5 copy-start.4
  223.3 109.9 %all-to-all-start.2 = ((f32[4,48,96,96]{3,1,0,2:T(8,128)}), f32[4,48,96,96]{3,1,0,2:T(8,128)}, u32[]{:S(2)}, u32[]{:S(2)}) async-start(f32[4,48,96,96]{3,1,0,2:T(8,128)} %copy.63), calls=%async_computation.2 | async-start | bytes 18874368 | tf_op jit(solution)/shard_map/all_to_all | solution.py:87
  240.5 8.3 copy-start.10
  240.5 8.3 copy-start.12
  240.5 8.3 copy-start.13
  333.3 108.9 %all-to-all-start = ((f32[4,48,96,96]{3,1,0,2:T(8,128)}), f32[4,48,96,96]{3,1,0,2:T(8,128)}, u32[]{:S(2)}, u32[]{:S(2)}) async-start(f32[4,48,96,96]{3,1,0,2:T(8,128)} %copy.47), calls=%async_computation | async-start | bytes 18874368 | tf_op jit(solution)/shard_map/all_to_all | solution.py:87
  363.5 11.1 %copy-start = (f32[4,96,48,96]{1,3,2,0:T(8,128)S(1)}, f32[4,96,48,96]{1,3,2,0:T(8,128)}, u32[]{:S(2)}) copy-start(f32[4,96,48,96]{1,3,2,0:T(8,128)} %copy.66) | copy-start | bytes 21233668
  442.2 108.3 %all-to-all-start.3 = ((f32[4,96,48,96]{3,2,0,1:T(8,128)}), f32[4,96,48,96]{3,2,0,1:T(8,128)}, u32[]{:S(2)}, u32[]{:S(2)}) async-start(f32[4,96,48,96]{3,2,0,1:T(8,128)} %copy.68), calls=%async_computation.3 | async-start | bytes 18874368 | tf_op jit(solution)/shard_map/all_to_all | solution.py:90
  472.8 11.1 %copy-start.1 = (f32[4,96,48,96]{1,3,2,0:T(8,128)S(1)}, f32[4,96,48,96]{1,3,2,0:T(8,128)}, u32[]{:S(2)}) copy-start(f32[4,96,48,96]{1,3,2,0:T(8,128)} %copy.50) | copy-start | bytes 21233668
  550.5 107.2 %all-to-all-start.1 = ((f32[4,96,48,96]{3,2,0,1:T(8,128)}), f32[4,96,48,96]{3,2,0,1:T(8,128)}, u32[]{:S(2)}, u32[]{:S(2)}) async-start(f32[4,96,48,96]{3,2,0,1:T(8,128)} %copy.52), calls=%async_computation.1 | async-start | bytes 18874368 | tf_op jit(solution)/shard_map/all_to_all | solution.py:90
  557.9 372.6 %all-reduce.5.cloned.1.call-start = ((), (), s32[]{:S(2)}) async-start(), calls=%async_computation.4 | async-start | bytes 7077888 | tf_op jit(solution)/shard_map/psum | solution.py:105
  662.9 36.5 %slice-start = ((s8[9437184]{0:T(1024)(128)(4,1)}), s8[4194304]{0:T(1024)(128)(4,1)S(1)}, s32[]{:S(2)}) async-start(s8[9437184]{0:T(1024)(128)(4,1)} %bitcast.148), calls=%async_computation.6 | async-start | bytes 8388608
  662.9 36.5 %slice-start.1 = ((s8[9437184]{0:T(1024)(128)(4,1)}), s8[4194304]{0:T(1024)(128)(4,1)S(1)}, s32[]{:S(2)}) async-start(s8[9437184]{0:T(1024)(128)(4,1)} %bitcast.148), calls=%async_computation.7 | async-start | bytes 8388608
  662.9 36.5 %slice-start.3 = ((s8[9437184]{0:T(1024)(128)(4,1)}), s8[4194304]{0:T(1024)(128)(4,1)S(1)}, s32[]{:S(2)}) async-start(s8[9437184]{0:T(1024)(128)(4,1)} %bitcast.150), calls=%async_computation.9 | async-start | bytes 8388608
  662.9 36.5 %slice-start.4 = ((s8[9437184]{0:T(1024)(128)(4,1)}), s8[4194304]{0:T(1024)(128)(4,1)S(1)}, s32[]{:S(2)}) async-start(s8[9437184]{0:T(1024)(128)(4,1)} %bitcast.150), calls=%async_computation.10 | async-start | bytes 8388608
  681.2 18.2 %slice-start.2 = ((s8[9437184]{0:T(1024)(128)(4,1)}), s8[1048576]{0:T(1024)(128)(4,1)S(1)}, s32[]{:S(2)}) async-start(s8[9437184]{0:T(1024)(128)(4,1)} %bitcast.148), calls=%async_computation.8 | async-start | bytes 2097152
  681.2 18.2 %slice-start.5 = ((s8[9437184]{0:T(1024)(128)(4,1)}), s8[1048576]{0:T(1024)(128)(4,1)S(1)}, s32[]{:S(2)}) async-start(s8[9437184]{0:T(1024)(128)(4,1)} %bitcast.150), calls=%async_computation.11 | async-start | bytes 2097152
  699.5 4.7 copy-start.11
  804.3 10.6 %copy-start.3 = (f32[4,48,4608]{2,1,0:T(8,128)S(1)}, f32[4,48,4608]{2,1,0:T(8,128)}, u32[]{:S(2)}) copy-start(f32[4,48,4608]{2,1,0:T(8,128)} %param.5) | copy-start | bytes 10616836
Sparse Core Ops, SparseCore 0:
  21.0 108.8 all-reduce.6
  827.1 103.3 all-reduce.4
where the time goes:
time: 953 us; the launch traced here: 942 us
  waiting for transfers between devices  299 us (31%)
  matrix products  269 us (28%)
  local copies, waits for them, and re-layouts  225 us (24%)
  other arithmetic  103 us (11%)
  starting transfers between devices  29.7 us (3%)
  between operations  16.2 us (2%)
    psum x1, waiting for transfers between devices, broadcast(): return lax.psum(jnp.where(mine, x, jnp.zeros_like(x)), axis)  108 us
    psum x1, waiting for transfers between devices, per_device(): collected.append(lax.psum(local_sum, 'band'))  104 us
    dot_general x8, matrix products, along_axis(): jnp.einsum(pattern, sine_table, values, precision=lax.Precision.HIGHEST)  100 us
    dot_general x8, matrix products, along_axis(): jnp.einsum(pattern, cosines, values, precision=lax.Precision.HIGHEST)  95.3 us
    dot_general x4, matrix products, along_last(): return jnp.matmul(values, matrix, precision=lax.Precision.HIGHEST)  73.1 us
    all_to_all x2, waiting for transfers between devices, per_device(): lax.all_to_all(columns, 'slab', split_axis=1, concat_axis=2, tiled=True)  67.9 us
    add x8, other arithmetic, along_axis(): real_part = with_cos[..., :middle] + with_sin[..., middle:]  46 us
    all_to_all x4, local copies, waits for them, and re-layouts, per_device(): lax.all_to_all(fields, 'slab', split_axis=2, concat_axis=1, tiled=True)  46 us
  transfers between devices with their start and end apart: 6, of which 6 were waited for; matrix products, arithmetic and copies ran while one was open for 34% of the time, Pallas kernels for 0%

commit v1 on v0

--- a/solution.py
+++ b/solution.py
@@ -1,20 +1,290 @@
+import functools
 import math
 
 import jax
 import jax.numpy as jnp
+import numpy as np
 from jax import lax
+from jax.experimental import pallas as pl
+from jax.experimental.pallas import tpu as pltpu
 from jax.sharding import PartitionSpec as P
 
 NX = 48
 NY = 96
 NZ = 96
 STEPS = 2
+OUTER = 12
+INNER = 8
+WIDE = INNER * NX
+SIN60 = math.sqrt(3.0) / 2.0
 
 
 length_first = 41.05
 length_side = 41.05
 length_last = 20.525
 omega_screen = 0.106
+
+
+def split_table(table):
+    high = table.astype(jnp.bfloat16)
+    low = (table - high.astype(np.float64)).astype(jnp.bfloat16)
+    return high, low
+
+
+def unit_table(rows, columns, length):
+    angle = 2.0 * np.pi / length * (np.outer(rows, columns) % length)
+    return np.cos(angle), np.sin(angle)
+
+
+def plane_table():
+    cy, sy = unit_table(np.arange(INNER), np.arange(INNER), INNER)
+    cx, sx = unit_table(np.arange(NX), np.arange(NX), NX)
+    cosines = np.kron(cy, cx) - np.kron(sy, sx)
+    sines = np.kron(cy, sx) + np.kron(sy, cx)
+    high, low = split_table(np.block([[cosines, -sines], [sines, cosines]]))
+    return np.concatenate([high, high, low], axis=0)
+
+
+def first_table(direction):
+    cosines, sines = unit_table(np.arange(NZ), np.arange(NZ), NZ)
+    sines = direction * sines
+    high, low = split_table(np.block([[cosines, sines], [-sines, cosines]]))
+    return np.concatenate([high, low, high], axis=1)
+
+
+def twiddle_table():
+    cosines, sines = unit_table(np.arange(OUTER), np.repeat(np.arange(INNER), NX), NY)
+    return np.stack([cosines, sines]).astype(np.float32)
+
+
+def screened_table():
+    def signed(length):
+        counter = np.arange(length)
+        return np.where(counter <= length // 2, counter, counter - length).astype(np.float64)
+
+    gz = 2.0 * math.pi / length_first * signed(NZ)
+    gy = 2.0 * math.pi / length_side * signed(NY)
+    gx = 2.0 * math.pi / length_last * signed(NX)
+    squared = gz[:, None, None] ** 2 + gy[None, :, None] ** 2 + gx[None, None, :] ** 2
+    safe = np.where(squared > 0, squared, 1.0)
+    screened = -4.0 * math.pi * np.expm1(-squared / (4.0 * omega_screen**2)) / safe
+    kernel = np.where(squared > 0, screened, math.pi / omega_screen**2) / (NX * NY * NZ)
+    kernel = kernel.reshape(NZ, INNER, OUTER, NX).transpose(2, 0, 1, 3)
+    return kernel.reshape(OUTER * NZ, WIDE).astype(np.float32)
+
+
+def transform3(parts):
+    (r0, i0), (r1, i1), (r2, i2) = parts
+    sr, si = r1 + r2, i1 + i2
+    dr, di = SIN60 * (r1 - r2), SIN60 * (i1 - i2)
+    mr, mi = r0 - 0.5 * sr, i0 - 0.5 * si
+    return [(r0 + sr, i0 + si), (mr + di, mi - dr), (mr - di, mi + dr)]
+
+
+def transform4(parts):
+    (r0, i0), (r1, i1), (r2, i2), (r3, i3) = parts
+    ar, ai, br, bi = r0 + r2, i0 + i2, r0 - r2, i0 - i2
+    cr, ci, dr, di = r1 + r3, i1 + i3, r1 - r3, i1 - i3
+    return [(ar + cr, ai + ci), (br + di, bi - dr), (ar - cr, ai - ci), (br - di, bi + dr)]
+
+
+def transform12(values):
+    rows = []
+    for n2 in range(4):
+        rows.append(transform3([values[(4 * n1 + 3 * n2) % 12] for n1 in range(3)]))
+    out = [None] * 12
+    for k1 in range(3):
+        column = transform4([rows[n2][k1] for n2 in range(4)])
+        for k2 in range(4):
+            out[(4 * k1 + 9 * k2) % 12] = column[k2]
+    return out
+
+
+def swapped(values):
+    return [(im, re) for re, im in values]
+
+
+def halves(value):
+    high = value.astype(jnp.bfloat16)
+    return high, (value - high.astype(jnp.float32)).astype(jnp.bfloat16)
+
+
+def put(split_ref, rows, column, value):
+    high, low = halves(value)
+    width = value.shape[-1]
+    split_ref[rows, pl.ds(column, width)] = high
+    split_ref[rows, pl.ds(2 * WIDE + column, width)] = low
+    split_ref[rows, pl.ds(4 * WIDE + column, width)] = high
+
+
+def potential_kernel(has_previous, *refs):
+    refs = list(refs)
+    plane_ref, forth_ref, back_ref, twiddle_ref, screen_ref = refs[:5]
+    orbital_refs, chosen_refs = refs[5:7], refs[7:9]
+    at = 9
+    previous_refs = [None, None]
+    if has_previous:
+        previous_refs = refs[at : at + 2]
+        at += 2
+    applied_refs, summed_refs = refs[at : at + 2], refs[at + 2 : at + 4]
+    split_ref, field_ref = refs[at + 4 : at + 6]
+    planes = orbital_refs[0].shape[1]
+    tall = 16
+
+    for part in range(2):
+        for lane in range(0, WIDE, 128):
+
+            @pl.loop(0, planes // tall)
+            def _(step, part=part, lane=lane):
+                start = pl.multiple_of(step * tall, tall)
+                here = pl.ds(start, tall)
+                values = []
+                for outer in range(OUTER):
+                    cols = pl.ds(outer * WIDE + lane, 128)
+                    orbital = orbital_refs[part][0, here, cols]
+                    values.append((orbital * chosen_refs[part][0, here, cols], orbital * chosen_refs[part][1, here, cols]))
+                for k1, (re, im) in enumerate(transform12(values)):
+                    if k1:
+                        tc = twiddle_ref[0, pl.ds(k1, 1), pl.ds(lane, 128)]
+                        ts = twiddle_ref[1, pl.ds(k1, 1), pl.ds(lane, 128)]
+                        re, im = re * tc + im * ts, im * tc - re * ts
+                    rows = pl.ds(pl.multiple_of(k1 * NZ + part * planes + start, tall), tall)
+                    put(split_ref, rows, lane, re)
+                    put(split_ref, rows, WIDE + lane, im)
+
+    def plane_pass():
+        chunk = 384
+
+        @pl.loop(0, OUTER * NZ // chunk)
+        def _(step):
+            rows = pl.ds(pl.multiple_of(step * chunk, chunk), chunk)
+            field_ref[rows, :] = jnp.dot(split_ref[rows, :], plane_ref[...], preferred_element_type=jnp.float32)
+
+    plane_pass()
+
+    @pl.loop(0, OUTER)
+    def _(k1):
+        rows = pl.ds(pl.multiple_of(k1 * NZ, NZ), NZ)
+        field = jnp.concatenate([field_ref[rows, :WIDE], field_ref[rows, WIDE:]], axis=0)
+        high, low = halves(field)
+        field = jnp.dot(forth_ref[...], jnp.concatenate([high, high, low], axis=0), preferred_element_type=jnp.float32)
+        screen = screen_ref[rows, :]
+        field = field * jnp.concatenate([screen, screen], axis=0)
+        high, low = halves(field)
+        field = jnp.dot(back_ref[...], jnp.concatenate([high, high, low], axis=0), preferred_element_type=jnp.float32)
+        put(split_ref, rows, 0, field[NZ:])
+        put(split_ref, rows, WIDE, field[:NZ])
+
+    plane_pass()
+
+    @pl.when(pl.program_id(0) == 0)
+    def _():
+        for summed_ref in summed_refs:
+            summed_ref[...] = jnp.zeros_like(summed_ref)
+
+    for part in range(2):
+        for lane in range(0, WIDE, 128):
+
+            @pl.loop(0, planes // 8)
+            def _(step, part=part, lane=lane):
+                start = pl.multiple_of(step * 8, 8)
+                here = pl.ds(start, 8)
+                values = []
+                for k1 in range(OUTER):
+                    rows = pl.ds(pl.multiple_of(k1 * NZ + part * planes + start, 8), 8)
+                    im = field_ref[rows, pl.ds(lane, 128)]
+                    re = field_ref[rows, pl.ds(WIDE + lane, 128)]
+                    if k1:
+                        tc = twiddle_ref[0, pl.ds(k1, 1), pl.ds(lane, 128)]
+                        ts = twiddle_ref[1, pl.ds(k1, 1), pl.ds(lane, 128)]
+                        re, im = re * tc - im * ts, re * ts + im * tc
+                    values.append((re, im))
+                for outer, (first, second) in enumerate(swapped(transform12(swapped(values)))):
+                    cols = pl.ds(outer * WIDE + lane, 128)
+                    orbital = orbital_refs[part][0, here, cols]
+                    applied = first * chosen_refs[part][0, here, cols] + second * chosen_refs[part][1, here, cols]
+                    if has_previous:
+                        applied = applied + previous_refs[part][0, here, cols]
+                    applied_refs[part][0, here, cols] = applied
+                    summed_refs[part][0, here, cols] += first * orbital
+                    summed_refs[part][1, here, cols] += second * orbital
+
+
+def potentials(orbital_parts, chosen_parts, previous_parts):
+    count, planes, points = orbital_parts[0].shape
+    tables = [plane_table(), first_table(1.0), first_table(-1.0), twiddle_table(), screened_table()]
+    tables = [jnp.asarray(table) for table in tables]
+    has_previous = previous_parts is not None
+
+    def whole(shape):
+        return pl.BlockSpec(shape, lambda band: (0,) * len(shape))
+
+    per_band = pl.BlockSpec((1, planes, points), lambda band: (band, 0, 0))
+    pair = whole((2, planes, points))
+    inputs = tables + list(orbital_parts) + list(chosen_parts) + (list(previous_parts) if has_previous else [])
+    in_specs = [whole(table.shape) for table in tables] + [per_band] * 2 + [pair] * 2 + [per_band] * (2 * has_previous)
+    band_shape = jax.ShapeDtypeStruct((count, planes, points), jnp.float32)
+    pair_shape = jax.ShapeDtypeStruct((2, planes, points), jnp.float32)
+    rows = OUTER * NZ
+    flops = count * (2 * 2 * rows * 6 * WIDE * 2 * WIDE + 2 * 2 * 2 * NZ * 6 * NZ * OUTER * WIDE)
+    moved = 4 * planes * points * (2 * count * (2 + has_previous) + 8 + 2)
+    return pl.pallas_call(
+        functools.partial(potential_kernel, has_previous),
+        grid=(count,),
+        out_shape=[band_shape] * 2 + [pair_shape] * 2,
+        in_specs=in_specs,
+        out_specs=[per_band] * 2 + [pair] * 2,
+        scratch_shapes=[
+            pltpu.VMEM((rows, 6 * WIDE), jnp.bfloat16),
+            pltpu.VMEM((rows, 2 * WIDE), jnp.float32),
+        ],
+        compiler_params=pltpu.CompilerParams(vmem_limit_bytes=56 * 1024 * 1024, dimension_semantics=("arbitrary",)),
+        cost_estimate=pl.CostEstimate(flops=2 * flops, bytes_accessed=moved, transcendentals=0),
+    )(*inputs)
+
+
+def whole_bands(orbitals, owner, picks):
+    bloc, planes, points = orbitals.shape
+    half = bloc // 2
+    slab = lax.axis_index("slab")
+    band = lax.axis_index("band")
+    core = lax.rem(band, 2)
+    groups = lax.axis_size("band")
+    across = [(0, 1), (1, 0)]
+    cores = [(index, index ^ 1) for index in range(groups)]
+
+    chosen = []
+    for step in range(STEPS):
+        fetched = jnp.take(orbitals, picks[step], axis=0)
+        fetched = jnp.where(band == owner[step], fetched, jnp.zeros_like(fetched))
+        if chosen:
+            fetched, chosen[-1] = lax.optimization_barrier((fetched, chosen[-1]))
+        chosen.append(lax.psum(fetched, "band"))
+
+    own = lax.dynamic_slice_in_dim(orbitals, slab * half, half, 0)
+    sent = lax.dynamic_slice_in_dim(orbitals, (1 - slab) * half, half, 0)
+    orbital_parts = (own, lax.ppermute(sent, "slab", across))
+
+    applied = None
+    collected = []
+    for step in range(STEPS):
+        row = lax.dynamic_index_in_dim(chosen[step], core, 0, keepdims=False)
+        row = lax.ppermute(row, "slab", across)
+        twin = lax.ppermute(row, "band", cores)
+        other = jnp.where(core == 0, jnp.stack([row, twin]), jnp.stack([twin, row]))
+        applied_own, applied_other, summed_own, summed_other = potentials(orbital_parts, (chosen[step], other), applied)
+        applied = (applied_own, applied_other)
+        keep = lax.dynamic_index_in_dim(summed_other, core, 0, keepdims=False)
+        give = lax.dynamic_index_in_dim(summed_other, 1 - core, 0, keepdims=False)
+        row = lax.ppermute(keep + lax.ppermute(give, "band", cores), "slab", across)
+        placed = jnp.where((jnp.arange(2) == core)[:, None, None], row[None], jnp.zeros_like(row)[None])
+        total = summed_own + placed
+        if collected:
+            total, collected[-1] = lax.optimization_barrier((total, collected[-1]))
+        collected.append(lax.psum(total, "band"))
+    back = lax.ppermute(applied[1], "slab", across)
+    exchange = jnp.where(slab == 0, jnp.concatenate([applied[0], back]), jnp.concatenate([back, applied[0]]))
+    return exchange, jnp.stack(collected)
 
 
 def broadcast(x, axis, root):
@@ -108,8 +378,7 @@
 
 
 def solution(mesh):
+    body = whole_bands if mesh.shape["slab"] == 2 and mesh.shape["band"] % 2 == 0 else per_device
     in_specs = (P("band", "slab", None), P(), P())
     out_specs = (P("band", "slab", None), P(None, None, "slab", None))
-    return jax.shard_map(
-        per_device, mesh=mesh, in_specs=in_specs, out_specs=out_specs, check_vma=False
-    )
+    return jax.shard_map(body, mesh=mesh, in_specs=in_specs, out_specs=out_specs, check_vma=False)

time: 953 us -> 565 us (0.59); the launches traced: 942 us -> 564 us
  matrix products: 269 us -> 0 us
  local copies, waits for them, and re-layouts: 225 us -> 16.8 us
  waiting for transfers between devices: 299 us -> 406 us
  Pallas kernels: 0 us -> 96.3 us
  other arithmetic: 103 us -> 22 us
  starting transfers between devices: 29.7 us -> 7.65 us
    dot_general x20 -> x0, matrix products: 269 us -> none  [the longest x8 100 us: along_axis(): jnp.einsum(pattern, sine_table, values, precision=lax.Precision.HIGHEST)]
    ppermute x0 -> x10, waiting for transfers between devices: none -> 153 us  [the longest x4 45.4 us: whole_bands(): row = lax.ppermute(keep + lax.ppermute(give, 'band', cores), 'slab', across)]
    pallas_call x0 -> x2, Pallas kernels: none -> 96.3 us  [potentials(): pl.pallas_call(functools.partial(potential_kernel, has_previous), grid=(c...]
    all_to_all x4 -> x0, waiting for transfers between devices: 88.2 us -> none  [the longest x2 67.9 us: per_device(): lax.all_to_all(columns, 'slab', split_axis=1, concat_axis=2, tiled=True)]
    reshape x8 -> x0, local copies, waits for them, and re-layouts: 73 us -> none  [the longest x2 20.9 us: per_device(): potentials_second_part = fields[..., NX:].reshape(count, planes, points)]
    all_to_all x6 -> x0, local copies, waits for them, and re-layouts: 56.2 us -> none  [the longest x4 46 us: per_device(): lax.all_to_all(fields, 'slab', split_axis=2, concat_axis=1, tiled=True)]
    concatenate x4 -> x0, local copies, waits for them, and re-layouts: 45.6 us -> none  [along_axis(): return jnp.concatenate([real_part, imag_part], axis=-1)]
    add x9 -> x4, other arithmetic: 46.1 us -> 3.06 us  [the longest x2 2.88 us: whole_bands(): total = summed_own + placed]
  transfers between devices with their start and end apart: 6 -> 13, of which waited for: 6 -> 13; matrix products, arithmetic and copies ran while one was open for 34% -> 3% of each run, Pallas kernels for 0% -> 0%
where the time goes in v1:
time: 565 us; the launch traced here: 564 us
  waiting for transfers between devices  406 us (72%)
  Pallas kernels  96.3 us (17%)
  other arithmetic  22 us (4%)
  local copies, waits for them, and re-layouts  16.8 us (3%)
  between operations  15.2 us (3%)
  starting transfers between devices  7.65 us (1%)
    psum x2, waiting for transfers between devices, whole_bands(): chosen.append(lax.psum(fetched, 'band'))  199 us
    pallas_call x2, Pallas kernels, potentials(): pl.pallas_call(functools.partial(potential_kernel, has_previous), grid=(c...  96.3 us
    psum x1, waiting for transfers between devices, whole_bands(): collected.append(lax.psum(total, 'band'))  54 us
    ppermute x4, waiting for transfers between devices, whole_bands(): row = lax.ppermute(keep + lax.ppermute(give, 'band', cores), 'slab', across)  45.4 us
    ppermute x2, waiting for transfers between devices, whole_bands(): row = lax.ppermute(row, 'slab', across)  37.2 us
    ppermute x1, waiting for transfers between devices, whole_bands(): back = lax.ppermute(applied[1], 'slab', across)  35.7 us
    ppermute x1, waiting for transfers between devices, whole_bands(): orbital_parts = (own, lax.ppermute(sent, 'slab', across))  30.1 us
  transfers between devices with their start and end apart: 13, of which 13 were waited for; matrix products, arithmetic and copies ran while one was open for 3% of the time, Pallas kernels for 0%

profile of v1, /device:TPU:0, one launch (start us, length us, event | category | flops | bytes accessed | tf_op | source)
XLA Modules:
  0.0 564.4 jit_solution(5267715629000830794)
XLA Ops:
  7.2 0.0 all-reduce.5.cloned.1.call-start
  7.2 1.4 fusion
  8.6 0.8 compare_and_fusion
  10.0 3.9 gather_fusion.1
  13.9 3.1 select_select_fusion
  17.0 0.0 all-reduce.9.cloned.1.call-start
  17.8 1.9 gather_fusion
  19.7 3.0 select_select_fusion.1
  22.6 93.7 %all-reduce.5.cloned.1.call-done.refs_7_ = f32[2,48,4608]{2,1,0:T(8,128)} async-done(((f32[2,48,4608]{2,1,0:T(8,128)}), f32[2,48,4608]{2,1,0:T(8,128)}) %all-reduce.5.cloned.1.call-update) | async-done | bytes 1769488 | tf_op jit(solution)/shard_map/psum | solution.py:262
  116.4 1.2 dynamic-slice_bitcast_fusion.2
  117.6 1.5 collective-permute-start.3
  119.1 2.1 constant_dynamic-slice_fusion
  121.2 0.6 collective-permute-start
  121.8 18.6 %collective-permute-done.3 = f32[48,4608]{1,0:T(8,128)} collective-permute-done((f32[48,4608]{1,0:T(8,128)S(1)}, f32[48,4608]{1,0:T(8,128)}, u32[]{:S(2)}, u32[]{:S(2)}) %collective-permute-start.3) | collective-permute-done | bytes 884768 | tf_op jit(solution)/shard_map/ppermute | solution.py:272
  140.4 2.6 collective-permute-done.4
  143.0 2.9 maximum_select_fusion.2.refs_8_
  145.9 30.1 %collective-permute-done.refs_6_ = f32[2,48,4608]{2,1,0:T(8,128)S(1)} collective-permute-done((f32[2,48,4608]{2,1,0:T(8,128)}, f32[2,48,4608]{2,1,0:T(8,128)S(1)}, u32[]{:S(2)}, u32[]{:S(2)}) %collective-permute-start) | collective-permute-done | bytes 1769504 | tf_op jit(solution)/shard_map/ppermute | solution.py:266
  175.9 1.2 copy-done.8
  177.1 47.7 %shard_map.140 = (f32[2,48,4608]{2,1,0:T(8,128)}, f32[2,48,4608]{2,1,0:T(8,128)}, f32[2,48,4608]{2,1,0:T(8,128)}, f32[2,48,4608]{2,1,0:T(8,128)}) custom-call(bf16[2304,768]{1,0:T(8,128)(2,1)} %constant.57.clone.refs_0_, bf16[192,576]{1,0:T(8,128)(2,1)} %constant.58.clone.refs_1_, bf16[192,576]{1,0:T(8,128)(2,1)} %constant.59.clone.refs_2_, ...), custom_call_target="tpu_custom_call" | custom-call | flops 40768634880 | bytes 15925248 | tf_op jit(solution)/shard_map/pallas_call | solution.py:231
  224.9 1.4 dynamic-slice_bitcast_fusion
  226.2 0.1 collective-permute-start.8
  226.3 2.4 collective-permute-done.8
  228.7 0.1 bitcast_add_fusion
  228.8 1.5 collective-permute-start.9
  230.4 20.2 %collective-permute-done.9 = f32[48,4608]{1,0:T(8,128)S(1)} collective-permute-done((f32[48,4608]{1,0:T(8,128)S(1)}, f32[48,4608]{1,0:T(8,128)S(1)}, u32[]{:S(2)}, u32[]{:S(2)}) %collective-permute-start.9) | collective-permute-done | bytes 884768 | tf_op jit(solution)/shard_map/ppermute | solution.py:279
  250.6 1.5 select_add_fusion
  252.0 0.0 all-reduce.9.cloned.1.call-update
  252.1 0.0 all-reduce.7.cloned.1.call-start
  252.1 105.3 %all-reduce.9.cloned.1.call-done = (f32[2,48,4608]{2,1,0:T(8,128)}, f32[2,48,4608]{2,1,0:T(8,128)}) async-done(((f32[2,48,4608]{2,1,0:T(8,128)}, f32[2,48,4608]{2,1,0:T(8,128)}), (f32[2,48,4608]{2,1,0:T(8,128)}, f32[2,48,4608]{2,1,0:T(8,128)})) %all-reduce.9.cloned.1.call-update) | async-done | bytes 3538960 | tf_op jit(solution)/shard_map/psum | solution.py:262
  357.4 1.2 dynamic-slice_bitcast_fusion.3
  358.6 1.5 collective-permute-start.1
  360.1 18.6 %collective-permute-done.1 = f32[48,4608]{1,0:T(8,128)S(1)} collective-permute-done((f32[48,4608]{1,0:T(8,128)S(1)}, f32[48,4608]{1,0:T(8,128)S(1)}, u32[]{:S(2)}, u32[]{:S(2)}) %collective-permute-start.1) | collective-permute-done | bytes 884768 | tf_op jit(solution)/shard_map/ppermute | solution.py:272
  378.8 2.4 collective-permute-done.2
  381.2 1.4 maximum_select_fusion.1.refs_8_
  382.6 48.6 %shard_map.141 = (f32[2,48,4608]{2,1,0:T(8,128)}, f32[2,48,4608]{2,1,0:T(8,128)}, f32[2,48,4608]{2,1,0:T(8,128)}, f32[2,48,4608]{2,1,0:T(8,128)}) custom-call(bf16[2304,768]{1,0:T(8,128)(2,1)} %constant.57.clone.refs_0_, bf16[192,576]{1,0:T(8,128)(2,1)} %constant.58.clone.refs_1_, bf16[192,576]{1,0:T(8,128)(2,1)} %constant.59.clone.refs_2_, ...), custom_call_target="tpu_custom_call" | custom-call | flops 40768634880 | bytes 19464192 | tf_op jit(solution)/shard_map/pallas_call | solution.py:231
  431.2 1.4 dynamic-slice_bitcast_fusion.1
  432.6 0.2 collective-permute-start.6
  432.8 2.3 collective-permute-done.6
  435.1 0.1 bitcast_add_fusion.1
  435.2 1.5 collective-permute-start.7
  436.7 0.6 collective-permute-start.5
  437.3 20.5 %collective-permute-done.7 = f32[48,4608]{1,0:T(8,128)S(1)} collective-permute-done((f32[48,4608]{1,0:T(8,128)S(1)}, f32[48,4608]{1,0:T(8,128)S(1)}, u32[]{:S(2)}, u32[]{:S(2)}) %collective-permute-start.7) | collective-permute-done | bytes 884768 | tf_op jit(solution)/shard_map/ppermute | solution.py:279
  457.8 1.4 select_add_fusion.1
  459.2 35.7 %collective-permute-done.5 = f32[2,48,4608]{2,1,0:T(8,128)S(1)} collective-permute-done((f32[2,48,4608]{2,1,0:T(8,128)}, f32[2,48,4608]{2,1,0:T(8,128)S(1)}, u32[]{:S(2)}, u32[]{:S(2)}) %collective-permute-start.5) | collective-permute-done | bytes 1769504 | tf_op jit(solution)/shard_map/ppermute | solution.py:285
  494.9 1.2 copy-done.3
  496.1 4.3 maximum_select_fusion
  500.3 54.0 %all-reduce.7.cloned.1.call-done = f32[1,2,48,4608]{3,2,1,0:T(8,128)} async-done(((f32[1,2,48,4608]{3,2,1,0:T(8,128)}), f32[1,2,48,4608]{3,2,1,0:T(8,128)}) %all-reduce.7.cloned.1.call-update) | async-done | bytes 1769488 | tf_op jit(solution)/shard_map/psum | solution.py:284
  554.3 3.5 pad_maximum_fusion
  (23 shorter events, 0.1 us)
Async XLA Ops:
  7.2 109.2 %all-reduce.5.cloned.1.call-start = ((), (), s32[]{:S(2)}) async-start(), calls=%async_computation | async-start | bytes 3538944 | tf_op jit(solution)/shard_map/psum | solution.py:262
  13.9 3.9 copy-start
  17.0 340.4 %all-reduce.9.cloned.1.call-start = ((), (), s32[]{:S(2)}) async-start(), calls=%async_computation.2 | async-start | bytes 7077888 | tf_op jit(solution)/shard_map/psum | solution.py:262
  117.6 22.8 %collective-permute-start.3 = (f32[48,4608]{1,0:T(8,128)S(1)}, f32[48,4608]{1,0:T(8,128)}, u32[]{:S(2)}, u32[]{:S(2)}) collective-permute-start(f32[48,4608]{1,0:T(8,128)S(1)} %dynamic-slice_bitcast_fusion.2), channel_id=1, source_target_pairs={{0,1},{1,0},{2,3},{3,2},{4,5},{5,4},{6,7},{7,6},{8,9},{9,8},{10,11... | collective-permute-start | bytes 2654216 | tf_op jit(solution)/shard_map/ppermute | solution.py:272
  121.2 54.7 %collective-permute-start = (f32[2,48,4608]{2,1,0:T(8,128)}, f32[2,48,4608]{2,1,0:T(8,128)S(1)}, u32[]{:S(2)}, u32[]{:S(2)}) collective-permute-start(f32[2,48,4608]{2,1,0:T(8,128)} %get-tuple-element.33), channel_id=1, source_target_pairs={{0,1},{1,0},{2,3},{3,2},{4,5},{5,4},{6,7},{7,6},{8,9},{9,8},{10,11... | collective-permute-start | bytes 5308424 | tf_op jit(solution)/shard_map/ppermute | solution.py:266
  140.4 2.6 collective-permute-start.4
  175.9 1.2 copy-start.8
  224.9 3.9 copy-start.7
  226.2 24.4 %copy-start.5 = (f32[2,48,4608]{2,1,0:T(8,128)S(1)}, f32[2,48,4608]{2,1,0:T(8,128)}, u32[]{:S(2)}) copy-start(f32[2,48,4608]{2,1,0:T(8,128)} %get-tuple-element.23) | copy-start | bytes 5308420
  226.2 2.5 collective-permute-start.8
  228.8 21.8 %collective-permute-start.9 = (f32[48,4608]{1,0:T(8,128)S(1)}, f32[48,4608]{1,0:T(8,128)S(1)}, u32[]{:S(2)}, u32[]{:S(2)}) collective-permute-start(f32[48,4608]{1,0:T(8,128)S(1)} %bitcast_add_fusion), channel_id=1, source_target_pairs={{0,1},{1,0},{2,3},{3,2},{4,5},{5,4},{6,7},{7,6},{8,9},{9,8},{10,11... | collective-permute-start | bytes 2654216 | tf_op jit(solution)/shard_map/ppermute | solution.py:279
  252.1 302.3 %all-reduce.7.cloned.1.call-start = ((), (), s32[]{:S(2)}) async-start(), calls=%async_computation.1 | async-start | bytes 3538944 | tf_op jit(solution)/shard_map/psum | solution.py:284
  358.6 20.2 %collective-permute-start.1 = (f32[48,4608]{1,0:T(8,128)S(1)}, f32[48,4608]{1,0:T(8,128)S(1)}, u32[]{:S(2)}, u32[]{:S(2)}) collective-permute-start(f32[48,4608]{1,0:T(8,128)S(1)} %dynamic-slice_bitcast_fusion.3), channel_id=1, source_target_pairs={{0,1},{1,0},{2,3},{3,2},{4,5},{5,4},{6,7},{7,6},{8,9},{9,8},{10,11... | collective-permute-start | bytes 2654216 | tf_op jit(solution)/shard_map/ppermute | solution.py:272
  378.8 2.4 collective-permute-start.2
  431.2 3.9 copy-start.6
  432.6 25.2 %copy-start.4 = (f32[2,48,4608]{2,1,0:T(8,128)S(1)}, f32[2,48,4608]{2,1,0:T(8,128)}, u32[]{:S(2)}) copy-start(f32[2,48,4608]{2,1,0:T(8,128)} %get-tuple-element.21) | copy-start | bytes 5308420
  432.6 2.5 collective-permute-start.6
  435.2 22.6 %collective-permute-start.7 = (f32[48,4608]{1,0:T(8,128)S(1)}, f32[48,4608]{1,0:T(8,128)S(1)}, u32[]{:S(2)}, u32[]{:S(2)}) collective-permute-start(f32[48,4608]{1,0:T(8,128)S(1)} %bitcast_add_fusion.1), channel_id=1, source_target_pairs={{0,1},{1,0},{2,3},{3,2},{4,5},{5,4},{6,7},{7,6},{8,9},{9,8},{10,11... | collective-permute-start | bytes 2654216 | tf_op jit(solution)/shard_map/ppermute | solution.py:279
  436.7 58.1 %collective-permute-start.5 = (f32[2,48,4608]{2,1,0:T(8,128)}, f32[2,48,4608]{2,1,0:T(8,128)S(1)}, u32[]{:S(2)}, u32[]{:S(2)}) collective-permute-start(f32[2,48,4608]{2,1,0:T(8,128)} %get-tuple-element.20), channel_id=1, source_target_pairs={{0,1},{1,0},{2,3},{3,2},{4,5},{5,4},{6,7},{7,6},{8,9},{9,8},{10,11... | collective-permute-start | bytes 5308424 | tf_op jit(solution)/shard_map/ppermute | solution.py:285
  459.2 36.9 %copy-start.2 = (f32[2,48,4608]{2,1,0:T(8,128)S(1)}, f32[2,48,4608]{2,1,0:T(8,128)}, u32[]{:S(2)}) copy-start(f32[2,48,4608]{2,1,0:T(8,128)} %get-tuple-element.19) | copy-start | bytes 5308420
  494.9 1.2 copy-start.3
  496.1 58.3 %copy-start.1 = (f32[2,48,4608]{2,1,0:T(8,128)S(1)}, f32[2,48,4608]{2,1,0:T(8,128)}, u32[]{:S(2)}) copy-start(f32[2,48,4608]{2,1,0:T(8,128)} %get-tuple-element.25) | copy-start | bytes 5308420
Sparse Core Ops, SparseCore 0:
  17.1 99.1 all-reduce.4
  252.2 105.1 all-reduce.8
  459.3 94.9 all-reduce.6

commit v2 on v1

--- a/solution.py
+++ b/solution.py
@@ -117,17 +117,12 @@
     split_ref[rows, pl.ds(4 * WIDE + column, width)] = high
 
 
-def potential_kernel(has_previous, *refs):
-    refs = list(refs)
+def potential_kernel(*refs):
     plane_ref, forth_ref, back_ref, twiddle_ref, screen_ref = refs[:5]
     orbital_refs, chosen_refs = refs[5:7], refs[7:9]
-    at = 9
-    previous_refs = [None, None]
-    if has_previous:
-        previous_refs = refs[at : at + 2]
-        at += 2
-    applied_refs, summed_refs = refs[at : at + 2], refs[at + 2 : at + 4]
-    split_ref, field_ref = refs[at + 4 : at + 6]
+    applied_refs, summed_refs = refs[9:11], refs[11:13]
+    split_ref, field_ref = refs[13:15]
+    turn = pl.program_id(1)
     planes = orbital_refs[0].shape[1]
     tall = 16
 
@@ -142,7 +137,7 @@
                 for outer in range(OUTER):
                     cols = pl.ds(outer * WIDE + lane, 128)
                     orbital = orbital_refs[part][0, here, cols]
-                    values.append((orbital * chosen_refs[part][0, here, cols], orbital * chosen_refs[part][1, here, cols]))
+                    values.append((orbital * chosen_refs[part][0, 0, 0, here, cols], orbital * chosen_refs[part][0, 0, 1, here, cols]))
                 for k1, (re, im) in enumerate(transform12(values)):
                     if k1:
                         tc = twiddle_ref[0, pl.ds(k1, 1), pl.ds(lane, 128)]
@@ -180,7 +175,7 @@
     @pl.when(pl.program_id(0) == 0)
     def _():
         for summed_ref in summed_refs:
-            summed_ref[...] = jnp.zeros_like(summed_ref)
+            summed_ref[turn] = jnp.zeros(summed_ref.shape[1:], jnp.float32)
 
     for part in range(2):
         for lane in range(0, WIDE, 128):
@@ -202,45 +197,191 @@
                 for outer, (first, second) in enumerate(swapped(transform12(swapped(values)))):
                     cols = pl.ds(outer * WIDE + lane, 128)
                     orbital = orbital_refs[part][0, here, cols]
-                    applied = first * chosen_refs[part][0, here, cols] + second * chosen_refs[part][1, here, cols]
-                    if has_previous:
-                        applied = applied + previous_refs[part][0, here, cols]
-                    applied_refs[part][0, here, cols] = applied
-                    summed_refs[part][0, here, cols] += first * orbital
-                    summed_refs[part][1, here, cols] += second * orbital
-
-
-def potentials(orbital_parts, chosen_parts, previous_parts):
+                    applied = first * chosen_refs[part][0, 0, 0, here, cols] + second * chosen_refs[part][0, 0, 1, here, cols]
+                    before = applied_refs[part][0, here, cols]
+                    applied_refs[part][0, here, cols] = jnp.where(turn == 0, applied, applied + before)
+                    summed_refs[part][turn, 0, here, cols] += first * orbital
+                    summed_refs[part][turn, 1, here, cols] += second * orbital
+
+
+def potentials(orbital_parts, chosen):
     count, planes, points = orbital_parts[0].shape
     tables = [plane_table(), first_table(1.0), first_table(-1.0), twiddle_table(), screened_table()]
     tables = [jnp.asarray(table) for table in tables]
-    has_previous = previous_parts is not None
-
-    def whole(shape):
-        return pl.BlockSpec(shape, lambda band: (0,) * len(shape))
-
-    per_band = pl.BlockSpec((1, planes, points), lambda band: (band, 0, 0))
-    pair = whole((2, planes, points))
-    inputs = tables + list(orbital_parts) + list(chosen_parts) + (list(previous_parts) if has_previous else [])
-    in_specs = [whole(table.shape) for table in tables] + [per_band] * 2 + [pair] * 2 + [per_band] * (2 * has_previous)
+
+    def constant(shape, **mode):
+        return pl.BlockSpec(shape, lambda band, turn: (0,) * len(shape), **mode)
+
+    def chosen_part(part):
+        return pl.BlockSpec((1, 1, 2, planes, points), lambda band, turn: (part, turn, 0, 0, 0))
+
+    per_band = pl.BlockSpec((1, planes, points), lambda band, turn: (band, 0, 0))
+    summed = (STEPS, 2, planes, points)
     band_shape = jax.ShapeDtypeStruct((count, planes, points), jnp.float32)
-    pair_shape = jax.ShapeDtypeStruct((2, planes, points), jnp.float32)
     rows = OUTER * NZ
-    flops = count * (2 * 2 * rows * 6 * WIDE * 2 * WIDE + 2 * 2 * 2 * NZ * 6 * NZ * OUTER * WIDE)
-    moved = 4 * planes * points * (2 * count * (2 + has_previous) + 8 + 2)
+    flops = STEPS * count * (2 * 2 * rows * 6 * WIDE * 2 * WIDE + 2 * 2 * 2 * NZ * 6 * NZ * OUTER * WIDE)
     return pl.pallas_call(
-        functools.partial(potential_kernel, has_previous),
-        grid=(count,),
-        out_shape=[band_shape] * 2 + [pair_shape] * 2,
-        in_specs=in_specs,
-        out_specs=[per_band] * 2 + [pair] * 2,
+        potential_kernel,
+        grid=(count, STEPS),
+        out_shape=[band_shape] * 2 + [jax.ShapeDtypeStruct(summed, jnp.float32)] * 2,
+        in_specs=[constant(table.shape, pipeline_mode=pl.Buffered(1)) for table in tables]
+        + [per_band] * 2
+        + [chosen_part(0), chosen_part(1)],
+        out_specs=[per_band] * 2 + [constant(summed)] * 2,
         scratch_shapes=[
             pltpu.VMEM((rows, 6 * WIDE), jnp.bfloat16),
             pltpu.VMEM((rows, 2 * WIDE), jnp.float32),
         ],
-        compiler_params=pltpu.CompilerParams(vmem_limit_bytes=56 * 1024 * 1024, dimension_semantics=("arbitrary",)),
-        cost_estimate=pl.CostEstimate(flops=2 * flops, bytes_accessed=moved, transcendentals=0),
-    )(*inputs)
+        compiler_params=pltpu.CompilerParams(
+            vmem_limit_bytes=56 * 1024 * 1024, dimension_semantics=("arbitrary", "arbitrary")
+        ),
+        cost_estimate=pl.CostEstimate(flops=flops, bytes_accessed=4 * planes * points * 32, transcendentals=0),
+    )(*tables, *orbital_parts, chosen, chosen)
+
+
+RING = 8
+BLOCKS = 4
+
+
+def ring_band(position, core):
+    x = position // 4
+    z = x * (7 - 2 * position) + position
+    return (z * 2 + x) * 2 + core
+
+
+def ring_kernel(slabs_in, slabs_out, *refs):
+    inputs = refs[: slabs_in * STEPS]
+    parcel_ref, out_ref, got_ref = refs[slabs_in * STEPS : slabs_in * STEPS + 3]
+    twin_ref, total_ref, ring_ref, cross_ref = refs[slabs_in * STEPS + 3 : slabs_in * STEPS + 7]
+    twin_send, twin_recv, ring_send, ring_recv, lone_send, lone_recv, gather_send, gather_recv, hand_send, hand_recv = refs[
+        slabs_in * STEPS + 7 :
+    ]
+    planes, points = inputs[0].shape[-2:]
+    half, width = planes // 2, points // BLOCKS
+    band, slab = lax.axis_index("band"), lax.axis_index("slab")
+    core, x, z = band % 2, (band // 2) % 2, band // 4
+    place = x * (7 - 2 * z) + z
+    twin = {"band": band + 1 - 2 * core}
+    across = {"slab": 1 - slab}
+    ends = [{"band": ring_band((place + 1) % RING, core)}, {"band": ring_band((place + RING - 1) % RING, core)}]
+
+    barrier = pltpu.get_barrier_semaphore()
+    for device in [twin, across] + ends:
+        pl.semaphore_signal(barrier, inc=1, device_id=device, device_id_type=pl.DeviceIdType.MESH)
+    pl.semaphore_wait(barrier, 4)
+
+    def push(source, target, send, recv, device):
+        copy = pltpu.make_async_remote_copy(
+            src_ref=source,
+            dst_ref=target,
+            send_sem=send,
+            recv_sem=recv,
+            device_id=device,
+            device_id_type=pl.DeviceIdType.MESH,
+        )
+        copy.start()
+        return copy
+
+    def spot(chunk, way):
+        lanes = pl.ds(pl.multiple_of((chunk % BLOCKS) * width, 128), width)
+        return chunk // BLOCKS, pl.ds(way * half, half), lanes
+
+    parcel = push(parcel_ref, got_ref, lone_send.at[0], lone_recv.at[0], across)
+
+    swaps = []
+    for at, ref in enumerate(inputs):
+        swaps.append(push(ref.at[1 - core], twin_ref.at[at], twin_send.at[at], twin_recv.at[at], twin))
+    for at, ref in enumerate(inputs):
+        swaps[at].wait_recv()
+        total_ref[at // STEPS, at % STEPS] = ref[core] + twin_ref[at]
+
+    hops = []
+    for hop in range(RING - 1):
+        for way in range(2):
+            sign = 1 - 2 * way
+            chunk = (place + sign * (-1 - hop) + 2 * RING) % RING
+            step, rows, lanes = spot(chunk, way)
+            source = total_ref.at[:, step, rows, lanes]
+            if hop:
+                hops[-2].wait_recv()
+                arrived = ring_ref.at[way, hop - 1]
+                arrived[...] += total_ref[:, step, rows, lanes]
+                source = arrived
+            hops.append(push(source, ring_ref.at[way, hop], ring_send.at[way, hop], ring_recv.at[way, hop], ends[way]))
+    step, _, lanes = spot(place, 0)
+    for way in range(2):
+        hops[-2 + way].wait_recv()
+        _, rows, _ = spot(place, way)
+        done = ring_ref[way, RING - 2] + total_ref[:, step, rows, lanes]
+        out_ref[0, step, core, rows, lanes] = done[0]
+        if slabs_in == 2:
+            cross_ref[0, rows, :] = done[1]
+    if slabs_in == 2:
+        crossing = push(cross_ref.at[0], cross_ref.at[1], lone_send.at[1], lone_recv.at[1], across)
+        crossing.wait_recv()
+        out_ref[0, step, core, :, lanes] += cross_ref[1]
+    else:
+        own = out_ref.at[0, step, core, :, lanes]
+        crossing = push(own, out_ref.at[1, step, core, :, lanes], lone_send.at[1], lone_recv.at[1], across)
+
+    hands = []
+    last = {}
+    for hop in range(RING):
+        for part in range(slabs_out):
+            if hop == 0 and part == 1:
+                crossing.wait_recv()
+            for way in range(2):
+                sign = 1 - 2 * way
+                step, rows, lanes = spot((place - sign * hop + RING) % RING, way)
+                if hop:
+                    last[part, way].wait_recv()
+                here = out_ref.at[part, step, core, rows, lanes]
+                if hop < RING - 1:
+                    copy = push(here, here, gather_send.at[part, way, hop], gather_recv.at[part, way, hop], ends[way])
+                    last[part, way] = copy
+                    hops.append(copy)
+                hands.append(push(here, here, hand_send.at[part, way, hop], hand_recv.at[part, way, hop], twin))
+    for copy in swaps + hops:
+        copy.wait_send()
+    crossing.wait_send()
+    for copy in hands:
+        copy.wait()
+    parcel.wait()
+
+
+def ring_sum(inputs, parcel, slabs_in, slabs_out, collective):
+    planes, points = inputs[0].shape[-2:]
+    half, width = planes // 2, points // BLOCKS
+    dma = pltpu.SemaphoreType.DMA
+    vmem = pl.BlockSpec(memory_space=pltpu.VMEM)
+    anywhere = pl.BlockSpec(memory_space=pl.ANY)
+    out = jax.ShapeDtypeStruct((slabs_out, STEPS, 2, planes, points), jnp.float32)
+    return pl.pallas_call(
+        functools.partial(ring_kernel, slabs_in, slabs_out),
+        out_shape=[out, jax.ShapeDtypeStruct(parcel.shape, jnp.float32)],
+        in_specs=[vmem] * len(inputs) + [anywhere],
+        out_specs=[vmem, anywhere],
+        scratch_shapes=[
+            pltpu.VMEM((len(inputs), planes, points), jnp.float32),
+            pltpu.VMEM((slabs_in, STEPS, planes, points), jnp.float32),
+            pltpu.VMEM((2, RING - 1, slabs_in, half, width), jnp.float32),
+            pltpu.VMEM((2, planes, width), jnp.float32),
+            dma((len(inputs),)),
+            dma((len(inputs),)),
+            dma((2, RING - 1)),
+            dma((2, RING - 1)),
+            dma((2,)),
+            dma((2,)),
+            dma((slabs_out, 2, RING - 1)),
+            dma((slabs_out, 2, RING - 1)),
+            dma((slabs_out, 2, RING)),
+            dma((slabs_out, 2, RING)),
+        ],
+        compiler_params=pltpu.CompilerParams(
+            collective_id=collective, has_side_effects=True, vmem_limit_bytes=48 * 1024 * 1024
+        ),
+        cost_estimate=pl.CostEstimate(flops=0, bytes_accessed=20 * planes * points * 4, transcendentals=0),
+    )(*inputs, parcel)
 
 
 def whole_bands(orbitals, owner, picks):
@@ -248,43 +389,18 @@
     half = bloc // 2
     slab = lax.axis_index("slab")
     band = lax.axis_index("band")
-    core = lax.rem(band, 2)
-    groups = lax.axis_size("band")
-    across = [(0, 1), (1, 0)]
-    cores = [(index, index ^ 1) for index in range(groups)]
-
-    chosen = []
+    fetched = []
     for step in range(STEPS):
-        fetched = jnp.take(orbitals, picks[step], axis=0)
-        fetched = jnp.where(band == owner[step], fetched, jnp.zeros_like(fetched))
-        if chosen:
-            fetched, chosen[-1] = lax.optimization_barrier((fetched, chosen[-1]))
-        chosen.append(lax.psum(fetched, "band"))
-
+        rows = jnp.stack([lax.dynamic_index_in_dim(orbitals, picks[step, row], 0, keepdims=False) for row in range(2)])
+        fetched.append(jnp.where(band == owner[step], rows, jnp.zeros_like(rows)))
     own = lax.dynamic_slice_in_dim(orbitals, slab * half, half, 0)
     sent = lax.dynamic_slice_in_dim(orbitals, (1 - slab) * half, half, 0)
-    orbital_parts = (own, lax.ppermute(sent, "slab", across))
-
-    applied = None
-    collected = []
-    for step in range(STEPS):
-        row = lax.dynamic_index_in_dim(chosen[step], core, 0, keepdims=False)
-        row = lax.ppermute(row, "slab", across)
-        twin = lax.ppermute(row, "band", cores)
-        other = jnp.where(core == 0, jnp.stack([row, twin]), jnp.stack([twin, row]))
-        applied_own, applied_other, summed_own, summed_other = potentials(orbital_parts, (chosen[step], other), applied)
-        applied = (applied_own, applied_other)
-        keep = lax.dynamic_index_in_dim(summed_other, core, 0, keepdims=False)
-        give = lax.dynamic_index_in_dim(summed_other, 1 - core, 0, keepdims=False)
-        row = lax.ppermute(keep + lax.ppermute(give, "band", cores), "slab", across)
-        placed = jnp.where((jnp.arange(2) == core)[:, None, None], row[None], jnp.zeros_like(row)[None])
-        total = summed_own + placed
-        if collected:
-            total, collected[-1] = lax.optimization_barrier((total, collected[-1]))
-        collected.append(lax.psum(total, "band"))
-    back = lax.ppermute(applied[1], "slab", across)
-    exchange = jnp.where(slab == 0, jnp.concatenate([applied[0], back]), jnp.concatenate([back, applied[0]]))
-    return exchange, jnp.stack(collected)
+    chosen, other = ring_sum(fetched, sent, 1, 2, 0)
+    applied_own, applied_other, summed_own, summed_other = potentials((own, other), chosen)
+    summed = [part[step] for part in (summed_own, summed_other) for step in range(STEPS)]
+    transposed, back = ring_sum(summed, applied_other, 2, 1, 1)
+    exchange = jnp.where(slab == 0, jnp.concatenate([applied_own, back]), jnp.concatenate([back, applied_own]))
+    return exchange, transposed[0]
 
 
 def broadcast(x, axis, root):
@@ -378,7 +494,7 @@
 
 
 def solution(mesh):
-    body = whole_bands if mesh.shape["slab"] == 2 and mesh.shape["band"] % 2 == 0 else per_device
+    body = whole_bands if (mesh.shape["band"], mesh.shape["slab"]) == (2 * RING, 2) else per_device
     in_specs = (P("band", "slab", None), P(), P())
     out_specs = (P("band", "slab", None), P(None, None, "slab", None))
     return jax.shard_map(body, mesh=mesh, in_specs=in_specs, out_specs=out_specs, check_vma=False)

time: 565 us -> 296 us (0.52)
  waiting for transfers between devices: 406 us -> 0 us
  Pallas kernels: 96.3 us -> 265 us
  other arithmetic: 22 us -> 2.35 us
  starting transfers between devices: 7.65 us -> 0 us
    psum x3 -> x0, waiting for transfers between devices: 253 us -> none  [the longest x2 199 us: whole_bands(): chosen.append(lax.psum(fetched, 'band'))]
    pallas_call x2 -> x3, Pallas kernels: 96.3 us -> 265 us  [the longest x2 174 us: ring_sum(): pl.pallas_call(functools.partial(ring_kernel, slabs_in, slabs_out), out_s...]
    ppermute x10 -> x0, waiting for transfers between devices: 153 us -> none  [the longest x4 45.4 us: whole_bands(): row = lax.ppermute(keep + lax.ppermute(give, 'band', cores), 'slab', across)]
    select_n x5 -> x2, other arithmetic: 14.6 us -> 2.35 us  [the longest x1 2.09 us: whole_bands(): jnp.where(slab == 0, jnp.concatenate([applied_own, back]), jnp.concatenat...]
    ppermute x10 -> x0, starting transfers between devices: 7.52 us -> none  [the longest x4 3.33 us: whole_bands(): row = lax.ppermute(keep + lax.ppermute(give, 'band', cores), 'slab', across)]
    gather x2 -> x0, local copies, waits for them, and re-layouts: 5.74 us -> none  [whole_bands(): fetched = jnp.take(orbitals, picks[step], axis=0)]
  transfers between devices with their start and end apart: 13 -> 0, of which waited for: 13 -> 0; matrix products, arithmetic and copies ran while one was open for 3% -> 0% of each run, Pallas kernels for 0% -> 0%
where the time goes in v2:
time: 296 us; the launch traced here: 295 us
  Pallas kernels  265 us (90%)
  local copies, waits for them, and re-layouts  18.1 us (6%)
  between operations  9.65 us (3%)
    pallas_call x2, Pallas kernels, ring_sum(): pl.pallas_call(functools.partial(ring_kernel, slabs_in, slabs_out), out_s...  174 us
    pallas_call x1, Pallas kernels, potentials(): pl.pallas_call(potential_kernel, grid=(count, STEPS), out_shape=[band_sha...  90.8 us
    unnamed x11, local copies, waits for them, and re-layouts  6.61 us

profile of v2, /device:TPU:0, one launch (start us, length us, event | category | flops | bytes accessed | tf_op | source)
XLA Modules:
  0.0 295.3 jit_solution(6352817679477170643)
XLA Ops:
  0.6 1.3 fusion.1
  3.3 1.5 fusion
  12.4 2.2 constant_dynamic-slice_fusion.2
  14.6 0.0 copy-start.1
  14.6 0.3 maximum_select_fusion.1
  14.9 1.7 copy-done.1
  16.6 2.1 constant_dynamic-slice_fusion
  18.6 87.2 %shard_map.95 = (f32[2,2,2,48,4608]{4,3,2,1,0:T(8,128)}, f32[2,48,4608]{2,1,0:T(8,128)S(1)}) custom-call(f32[2,48,4608]{2,1,0:T(8,128)S(1)} %get-tuple-element.34.refs_0_, f32[2,48,4608]{2,1,0:T(8,128)S(1)} %get-tuple-element.35.refs_1_, f32[2,48,4608]{2,1,0:T(8,128)} %get-tuple-element.22.refs_2_), custom_call_target="tpu_custom_call" | custom-call | bytes 17694720 | tf_op jit(solution)/shard_map/pallas_call | solution.py:359
  105.9 0.0 copy-start
  105.9 1.2 copy-done
  107.1 90.8 %shard_map.96 = (f32[2,48,4608]{2,1,0:T(8,128)}, f32[2,48,4608]{2,1,0:T(8,128)}, f32[2,2,48,4608]{3,2,1,0:T(8,128)}, f32[2,2,48,4608]{3,2,1,0:T(8,128)}) custom-call(bf16[2304,768]{1,0:T(8,128)(2,1)} %constant.38.clone.refs_0_, bf16[192,576]{1,0:T(8,128)(2,1)} %constant.39.clone.refs_1_, bf16[192,576]{1,0:T(8,128)(2,1)} %constant.40.clone.refs_2_, ...), custom_call_target="tpu_custom_call" | custom-call | flops 40768634880 | bytes 28311552 | tf_op jit(solution)/shard_map/pallas_call | solution.py:223
  197.9 0.0 copy-start.2
  197.9 2.4 slice_bitcast_fusion.2
  200.3 0.7 copy-done.2
  201.0 2.0 slice_bitcast_fusion
  203.0 0.0 copy-start.4
  203.0 87.2 %shard_map.97 = (f32[1,2,2,48,4608]{4,3,2,1,0:T(8,128)}, f32[2,48,4608]{2,1,0:T(8,128)S(1)}) custom-call(f32[2,48,4608]{2,1,0:T(8,128)S(1)} %get-tuple-element.21.refs_0_, f32[2,48,4608]{2,1,0:T(8,128)S(1)} %get-tuple-element.20.refs_1_, f32[2,48,4608]{2,1,0:T(8,128)} %get-tuple-element.19.refs_2_, f32[2,48,4608]{2,1,0:T(8,128)} %get-tuple-element.18.refs_3_, ...), custom_call_target="tpu_custom_call" | custom-call | bytes 17694720 | tf_op jit(solution)/shard_map/pallas_call | solution.py:359
  290.2 0.0 copy-done.4
  290.2 0.0 copy-start.3
  290.2 2.1 maximum_select_fusion
  292.3 1.2 copy-done.3
  293.5 1.8 copy.11
Async XLA Ops:
  14.6 2.0 copy-start.1
  105.9 1.2 copy-start
  197.9 3.1 %copy-start.2 = (f32[2,2,48,4608]{3,2,1,0:T(8,128)S(1)}, f32[2,2,48,4608]{3,2,1,0:T(8,128)}, u32[]{:S(2)}) copy-start(f32[2,2,48,4608]{3,2,1,0:T(8,128)} %get-tuple-element.14) | copy-start | bytes 10616836
  203.0 87.2 %copy-start.4 = (f32[2,48,4608]{2,1,0:T(8,128)S(1)}, f32[2,48,4608]{2,1,0:T(8,128)}, u32[]{:S(2)}) copy-start(f32[2,48,4608]{2,1,0:T(8,128)} %get-tuple-element.12) | copy-start | bytes 5308420
  290.2 3.3 %copy-start.3 = (f32[1,2,2,48,4608]{4,3,2,1,0:T(8,128)S(1)}, f32[1,2,2,48,4608]{4,3,2,1,0:T(8,128)}, u32[]{:S(2)}) copy-start(f32[1,2,2,48,4608]{4,3,2,1,0:T(8,128)} %get-tuple-element.17) | copy-start | bytes 10616836

commit v3 on v2

--- a/solution.py
+++ b/solution.py
@@ -117,35 +117,29 @@
     split_ref[rows, pl.ds(4 * WIDE + column, width)] = high
 
 
-def potential_kernel(*refs):
-    plane_ref, forth_ref, back_ref, twiddle_ref, screen_ref = refs[:5]
-    orbital_refs, chosen_refs = refs[5:7], refs[7:9]
-    applied_refs, summed_refs = refs[9:11], refs[11:13]
-    split_ref, field_ref = refs[13:15]
-    turn = pl.program_id(1)
-    planes = orbital_refs[0].shape[1]
+def potential_stages(tables, orbital_refs, chosen_ref, previous_refs, applied_refs, summed_refs, split_ref, field_ref):
+    plane_ref, forth_ref, back_ref, twiddle_ref, screen_ref = tables
+    bands, planes, _ = orbital_refs[0].shape
     tall = 16
 
-    for part in range(2):
-        for lane in range(0, WIDE, 128):
-
-            @pl.loop(0, planes // tall)
-            def _(step, part=part, lane=lane):
-                start = pl.multiple_of(step * tall, tall)
-                here = pl.ds(start, tall)
-                values = []
-                for outer in range(OUTER):
-                    cols = pl.ds(outer * WIDE + lane, 128)
-                    orbital = orbital_refs[part][0, here, cols]
-                    values.append((orbital * chosen_refs[part][0, 0, 0, here, cols], orbital * chosen_refs[part][0, 0, 1, here, cols]))
-                for k1, (re, im) in enumerate(transform12(values)):
-                    if k1:
-                        tc = twiddle_ref[0, pl.ds(k1, 1), pl.ds(lane, 128)]
-                        ts = twiddle_ref[1, pl.ds(k1, 1), pl.ds(lane, 128)]
-                        re, im = re * tc + im * ts, im * tc - re * ts
-                    rows = pl.ds(pl.multiple_of(k1 * NZ + part * planes + start, tall), tall)
-                    put(split_ref, rows, lane, re)
-                    put(split_ref, rows, WIDE + lane, im)
+    def pair_fields(band, part, lane):
+        @pl.loop(0, planes // tall)
+        def _(step):
+            start = pl.multiple_of(step * tall, tall)
+            here = pl.ds(start, tall)
+            values = []
+            for outer in range(OUTER):
+                cols = pl.ds(outer * WIDE + lane, 128)
+                orbital = orbital_refs[part][band, here, cols]
+                values.append((orbital * chosen_ref[part, 0, here, cols], orbital * chosen_ref[part, 1, here, cols]))
+            for k1, (re, im) in enumerate(transform12(values)):
+                if k1:
+                    tc = twiddle_ref[0, pl.ds(k1, 1), pl.ds(lane, 128)]
+                    ts = twiddle_ref[1, pl.ds(k1, 1), pl.ds(lane, 128)]
+                    re, im = re * tc + im * ts, im * tc - re * ts
+                rows = pl.ds(pl.multiple_of(k1 * NZ + part * planes + start, tall), tall)
+                put(split_ref, rows, lane, re)
+                put(split_ref, rows, WIDE + lane, im)
 
     def plane_pass():
         chunk = 384
@@ -155,88 +149,65 @@
             rows = pl.ds(pl.multiple_of(step * chunk, chunk), chunk)
             field_ref[rows, :] = jnp.dot(split_ref[rows, :], plane_ref[...], preferred_element_type=jnp.float32)
 
-    plane_pass()
-
-    @pl.loop(0, OUTER)
-    def _(k1):
-        rows = pl.ds(pl.multiple_of(k1 * NZ, NZ), NZ)
-        field = jnp.concatenate([field_ref[rows, :WIDE], field_ref[rows, WIDE:]], axis=0)
-        high, low = halves(field)
-        field = jnp.dot(forth_ref[...], jnp.concatenate([high, high, low], axis=0), preferred_element_type=jnp.float32)
-        screen = screen_ref[rows, :]
-        field = field * jnp.concatenate([screen, screen], axis=0)
-        high, low = halves(field)
-        field = jnp.dot(back_ref[...], jnp.concatenate([high, high, low], axis=0), preferred_element_type=jnp.float32)
-        put(split_ref, rows, 0, field[NZ:])
-        put(split_ref, rows, WIDE, field[:NZ])
-
-    plane_pass()
-
-    @pl.when(pl.program_id(0) == 0)
-    def _():
-        for summed_ref in summed_refs:
-            summed_ref[turn] = jnp.zeros(summed_ref.shape[1:], jnp.float32)
-
-    for part in range(2):
+    def screen_columns(first, last):
+        @pl.loop(first, last)
+        def _(k1):
+            rows = pl.ds(pl.multiple_of(k1 * NZ, NZ), NZ)
+            field = jnp.concatenate([field_ref[rows, :WIDE], field_ref[rows, WIDE:]], axis=0)
+            high, low = halves(field)
+            field = jnp.dot(forth_ref[...], jnp.concatenate([high, high, low], axis=0), preferred_element_type=jnp.float32)
+            screen = screen_ref[rows, :]
+            field = field * jnp.concatenate([screen, screen], axis=0)
+            high, low = halves(field)
+            field = jnp.dot(back_ref[...], jnp.concatenate([high, high, low], axis=0), preferred_element_type=jnp.float32)
+            put(split_ref, rows, 0, field[NZ:])
+            put(split_ref, rows, WIDE, field[:NZ])
+
+    def apply(band, part, lane):
+        @pl.loop(0, planes // 8)
+        def _(step):
+            start = pl.multiple_of(step * 8, 8)
+            here = pl.ds(start, 8)
+            values = []
+            for k1 in range(OUTER):
+                rows = pl.ds(pl.multiple_of(k1 * NZ + part * planes + start, 8), 8)
+                im = field_ref[rows, pl.ds(lane, 128)]
+                re = field_ref[rows, pl.ds(WIDE + lane, 128)]
+                if k1:
+                    tc = twiddle_ref[0, pl.ds(k1, 1), pl.ds(lane, 128)]
+                    ts = twiddle_ref[1, pl.ds(k1, 1), pl.ds(lane, 128)]
+                    re, im = re * tc - im * ts, re * ts + im * tc
+                values.append((re, im))
+            for outer, (first, second) in enumerate(swapped(transform12(swapped(values)))):
+                cols = pl.ds(outer * WIDE + lane, 128)
+                orbital = orbital_refs[part][band, here, cols]
+                applied = first * chosen_ref[part, 0, here, cols] + second * chosen_ref[part, 1, here, cols]
+                if previous_refs:
+                    applied = applied + previous_refs[part][band, here, cols]
+                applied_refs[part][band, here, cols] = applied
+                first, second = first * orbital, second * orbital
+                if band:
+                    first = first + summed_refs[part][0, here, cols]
+                    second = second + summed_refs[part][1, here, cols]
+                summed_refs[part][0, here, cols] = first
+                summed_refs[part][1, here, cols] = second
+
+    for band in range(bands):
         for lane in range(0, WIDE, 128):
-
-            @pl.loop(0, planes // 8)
-            def _(step, part=part, lane=lane):
-                start = pl.multiple_of(step * 8, 8)
-                here = pl.ds(start, 8)
-                values = []
-                for k1 in range(OUTER):
-                    rows = pl.ds(pl.multiple_of(k1 * NZ + part * planes + start, 8), 8)
-                    im = field_ref[rows, pl.ds(lane, 128)]
-                    re = field_ref[rows, pl.ds(WIDE + lane, 128)]
-                    if k1:
-                        tc = twiddle_ref[0, pl.ds(k1, 1), pl.ds(lane, 128)]
-                        ts = twiddle_ref[1, pl.ds(k1, 1), pl.ds(lane, 128)]
-                        re, im = re * tc - im * ts, re * ts + im * tc
-                    values.append((re, im))
-                for outer, (first, second) in enumerate(swapped(transform12(swapped(values)))):
-                    cols = pl.ds(outer * WIDE + lane, 128)
-                    orbital = orbital_refs[part][0, here, cols]
-                    applied = first * chosen_refs[part][0, 0, 0, here, cols] + second * chosen_refs[part][0, 0, 1, here, cols]
-                    before = applied_refs[part][0, here, cols]
-                    applied_refs[part][0, here, cols] = jnp.where(turn == 0, applied, applied + before)
-                    summed_refs[part][turn, 0, here, cols] += first * orbital
-                    summed_refs[part][turn, 1, here, cols] += second * orbital
-
-
-def potentials(orbital_parts, chosen):
-    count, planes, points = orbital_parts[0].shape
-    tables = [plane_table(), first_table(1.0), first_table(-1.0), twiddle_table(), screened_table()]
-    tables = [jnp.asarray(table) for table in tables]
-
-    def constant(shape, **mode):
-        return pl.BlockSpec(shape, lambda band, turn: (0,) * len(shape), **mode)
-
-    def chosen_part(part):
-        return pl.BlockSpec((1, 1, 2, planes, points), lambda band, turn: (part, turn, 0, 0, 0))
-
-    per_band = pl.BlockSpec((1, planes, points), lambda band, turn: (band, 0, 0))
-    summed = (STEPS, 2, planes, points)
-    band_shape = jax.ShapeDtypeStruct((count, planes, points), jnp.float32)
-    rows = OUTER * NZ
-    flops = STEPS * count * (2 * 2 * rows * 6 * WIDE * 2 * WIDE + 2 * 2 * 2 * NZ * 6 * NZ * OUTER * WIDE)
-    return pl.pallas_call(
-        potential_kernel,
-        grid=(count, STEPS),
-        out_shape=[band_shape] * 2 + [jax.ShapeDtypeStruct(summed, jnp.float32)] * 2,
-        in_specs=[constant(table.shape, pipeline_mode=pl.Buffered(1)) for table in tables]
-        + [per_band] * 2
-        + [chosen_part(0), chosen_part(1)],
-        out_specs=[per_band] * 2 + [constant(summed)] * 2,
-        scratch_shapes=[
-            pltpu.VMEM((rows, 6 * WIDE), jnp.bfloat16),
-            pltpu.VMEM((rows, 2 * WIDE), jnp.float32),
-        ],
-        compiler_params=pltpu.CompilerParams(
-            vmem_limit_bytes=56 * 1024 * 1024, dimension_semantics=("arbitrary", "arbitrary")
-        ),
-        cost_estimate=pl.CostEstimate(flops=flops, bytes_accessed=4 * planes * points * 32, transcendentals=0),
-    )(*tables, *orbital_parts, chosen, chosen)
+            pair_fields(band, 0, lane)
+            pair_fields(band, 1, lane)
+            yield
+        plane_pass()
+        yield
+        for first in range(0, OUTER, 4):
+            screen_columns(first, first + 4)
+            yield
+        plane_pass()
+        yield
+        for lane in range(0, WIDE, 128):
+            apply(band, 0, lane)
+            apply(band, 1, lane)
+            yield
 
 
 RING = 8
@@ -249,13 +220,15 @@
     return (z * 2 + x) * 2 + core
 
 
-def ring_kernel(slabs_in, slabs_out, *refs):
-    inputs = refs[: slabs_in * STEPS]
-    parcel_ref, out_ref, got_ref = refs[slabs_in * STEPS : slabs_in * STEPS + 3]
-    twin_ref, total_ref, ring_ref, cross_ref = refs[slabs_in * STEPS + 3 : slabs_in * STEPS + 7]
-    twin_send, twin_recv, ring_send, ring_recv, lone_send, lone_recv, gather_send, gather_recv, hand_send, hand_recv = refs[
-        slabs_in * STEPS + 7 :
-    ]
+def way_lanes(width):
+    first = (width // 128 + 1) // 2 * 128
+    return (0, first), (first, width - first)
+
+
+def ring_stages(inputs, parcel_ref, out_ref, got_ref, scratch):
+    twin_ref, total_ref, ring_ref, cross_ref = scratch[:4]
+    twin_send, twin_recv, ring_send, ring_recv, lone_send, lone_recv, gather_send, gather_recv, hand_send, hand_recv = scratch[4:]
+    slabs_in, slabs_out = len(inputs), out_ref.shape[0]
     planes, points = inputs[0].shape[-2:]
     half, width = planes // 2, points // BLOCKS
     band, slab = lax.axis_index("band"), lax.axis_index("slab")
@@ -283,91 +256,127 @@
         return copy
 
     def spot(chunk, way):
-        lanes = pl.ds(pl.multiple_of((chunk % BLOCKS) * width, 128), width)
-        return chunk // BLOCKS, pl.ds(way * half, half), lanes
-
-    parcel = push(parcel_ref, got_ref, lone_send.at[0], lone_recv.at[0], across)
+        offset, extent = way_lanes(width)[way]
+        lanes = pl.ds(pl.multiple_of((chunk % BLOCKS) * width + offset, 128), extent)
+        return pl.ds(pl.multiple_of(chunk // BLOCKS * half, 8), half), lanes
+
+    parcel = None
+    if parcel_ref is not None:
+        parcel = push(parcel_ref, got_ref, lone_send.at[0], lone_recv.at[0], across)
 
     swaps = []
     for at, ref in enumerate(inputs):
         swaps.append(push(ref.at[1 - core], twin_ref.at[at], twin_send.at[at], twin_recv.at[at], twin))
+    yield
     for at, ref in enumerate(inputs):
         swaps[at].wait_recv()
-        total_ref[at // STEPS, at % STEPS] = ref[core] + twin_ref[at]
+        total_ref[at] = ref[core] + twin_ref[at]
 
     hops = []
     for hop in range(RING - 1):
         for way in range(2):
             sign = 1 - 2 * way
             chunk = (place + sign * (-1 - hop) + 2 * RING) % RING
-            step, rows, lanes = spot(chunk, way)
-            source = total_ref.at[:, step, rows, lanes]
+            rows, lanes = spot(chunk, way)
+            extent = way_lanes(width)[way][1]
+            source = total_ref.at[:, rows, lanes]
             if hop:
                 hops[-2].wait_recv()
-                arrived = ring_ref.at[way, hop - 1]
-                arrived[...] += total_ref[:, step, rows, lanes]
+                arrived = ring_ref.at[way, hop - 1, :, :, pl.ds(0, extent)]
+                arrived[...] += total_ref[:, rows, lanes]
                 source = arrived
-            hops.append(push(source, ring_ref.at[way, hop], ring_send.at[way, hop], ring_recv.at[way, hop], ends[way]))
-    step, _, lanes = spot(place, 0)
+            target = ring_ref.at[way, hop, :, :, pl.ds(0, extent)]
+            hops.append(push(source, target, ring_send.at[way, hop], ring_recv.at[way, hop], ends[way]))
+        yield
     for way in range(2):
         hops[-2 + way].wait_recv()
-        _, rows, _ = spot(place, way)
-        done = ring_ref[way, RING - 2] + total_ref[:, step, rows, lanes]
-        out_ref[0, step, core, rows, lanes] = done[0]
+        rows, lanes = spot(place, way)
+        offset, extent = way_lanes(width)[way]
+        done = ring_ref[way, RING - 2, :, :, pl.ds(0, extent)] + total_ref[:, rows, lanes]
+        out_ref[0, core, rows, lanes] = done[0]
         if slabs_in == 2:
-            cross_ref[0, rows, :] = done[1]
+            cross_ref[0, :, pl.ds(offset, extent)] = done[1]
+    rows, _ = spot(place, 0)
+    lanes = pl.ds(pl.multiple_of(place % BLOCKS * width, 128), width)
+    own = out_ref.at[0, core, rows, lanes]
     if slabs_in == 2:
         crossing = push(cross_ref.at[0], cross_ref.at[1], lone_send.at[1], lone_recv.at[1], across)
+        yield
         crossing.wait_recv()
-        out_ref[0, step, core, :, lanes] += cross_ref[1]
+        own[...] += cross_ref[1]
     else:
-        own = out_ref.at[0, step, core, :, lanes]
-        crossing = push(own, out_ref.at[1, step, core, :, lanes], lone_send.at[1], lone_recv.at[1], across)
+        crossing = push(own, out_ref.at[1, core, rows, lanes], lone_send.at[1], lone_recv.at[1], across)
 
     hands = []
     last = {}
     for hop in range(RING):
         for part in range(slabs_out):
             if hop == 0 and part == 1:
+                yield
                 crossing.wait_recv()
             for way in range(2):
                 sign = 1 - 2 * way
-                step, rows, lanes = spot((place - sign * hop + RING) % RING, way)
+                rows, lanes = spot((place - sign * hop + RING) % RING, way)
                 if hop:
                     last[part, way].wait_recv()
-                here = out_ref.at[part, step, core, rows, lanes]
+                here = out_ref.at[part, core, rows, lanes]
                 if hop < RING - 1:
                     copy = push(here, here, gather_send.at[part, way, hop], gather_recv.at[part, way, hop], ends[way])
                     last[part, way] = copy
                     hops.append(copy)
                 hands.append(push(here, here, hand_send.at[part, way, hop], hand_recv.at[part, way, hop], twin))
-    for copy in swaps + hops:
+        yield
+    for copy in swaps + hops + [crossing]:
         copy.wait_send()
-    crossing.wait_send()
     for copy in hands:
         copy.wait()
-    parcel.wait()
-
-
-def ring_sum(inputs, parcel, slabs_in, slabs_out, collective):
-    planes, points = inputs[0].shape[-2:]
+    if parcel is not None:
+        parcel.wait()
+
+
+def step_kernel(counts, *refs):
+    refs = list(refs)
+    groups = []
+    for count in counts:
+        groups.append(refs[:count])
+        refs = refs[count:]
+    tables, orbitals, chosen, previous, inputs, parcel, applied, summed, out, got, fields, scratch = groups
+    ring = iter(()) if not inputs else ring_stages(inputs, parcel[0] if parcel else None, out[0], got[0] if got else None, scratch)
+    if tables:
+        for _ in potential_stages(tables, orbitals, chosen[0], previous, applied, summed, *fields):
+            next(ring, None)
+    for _ in ring:
+        pass
+
+
+def run_step(collective, orbitals=(), chosen=(), previous=(), inputs=(), parcel=()):
+    planes, points = (list(inputs) + list(orbitals))[0].shape[-2:]
     half, width = planes // 2, points // BLOCKS
+    slabs_in = len(inputs)
+    slabs_out = 3 - slabs_in
+    rows = OUTER * NZ
     dma = pltpu.SemaphoreType.DMA
     vmem = pl.BlockSpec(memory_space=pltpu.VMEM)
     anywhere = pl.BlockSpec(memory_space=pl.ANY)
-    out = jax.ShapeDtypeStruct((slabs_out, STEPS, 2, planes, points), jnp.float32)
-    return pl.pallas_call(
-        functools.partial(ring_kernel, slabs_in, slabs_out),
-        out_shape=[out, jax.ShapeDtypeStruct(parcel.shape, jnp.float32)],
-        in_specs=[vmem] * len(inputs) + [anywhere],
-        out_specs=[vmem, anywhere],
-        scratch_shapes=[
-            pltpu.VMEM((len(inputs), planes, points), jnp.float32),
-            pltpu.VMEM((slabs_in, STEPS, planes, points), jnp.float32),
-            pltpu.VMEM((2, RING - 1, slabs_in, half, width), jnp.float32),
-            pltpu.VMEM((2, planes, width), jnp.float32),
-            dma((len(inputs),)),
-            dma((len(inputs),)),
+    tables, shapes, fields, ring, flops = [], [], [], [], 0
+    pair = jax.ShapeDtypeStruct((2, planes, points), jnp.float32)
+    if orbitals:
+        tables = [plane_table(), first_table(1.0), first_table(-1.0), twiddle_table(), screened_table()]
+        tables = [jnp.asarray(table) for table in tables]
+        shapes = [jax.ShapeDtypeStruct(part.shape, jnp.float32) for part in orbitals] + [pair] * 2
+        fields = [pltpu.VMEM((rows, 6 * WIDE), jnp.bfloat16), pltpu.VMEM((rows, 2 * WIDE), jnp.float32)]
+        flops = 2 * (2 * 2 * rows * 6 * WIDE * 2 * WIDE + 2 * 2 * 2 * NZ * 6 * NZ * OUTER * WIDE)
+    specs = [vmem] * len(shapes)
+    if inputs:
+        shapes.append(jax.ShapeDtypeStruct((slabs_out, 2, planes, points), jnp.float32))
+        specs.append(vmem)
+        ring = [
+            pltpu.VMEM((slabs_in, planes, points), jnp.float32),
+            pltpu.VMEM((slabs_in, planes, points), jnp.float32),
+            pltpu.VMEM((2, RING - 1, slabs_in, half, way_lanes(width)[0][1]), jnp.float32),
+            pltpu.VMEM((2, half, width), jnp.float32),
+            dma((slabs_in,)),
+            dma((slabs_in,)),
             dma((2, RING - 1)),
             dma((2, RING - 1)),
             dma((2,)),
@@ -376,12 +385,25 @@
             dma((slabs_out, 2, RING - 1)),
             dma((slabs_out, 2, RING)),
             dma((slabs_out, 2, RING)),
-        ],
+        ]
+    for part in parcel:
+        shapes.append(jax.ShapeDtypeStruct(part.shape, jnp.float32))
+        specs.append(anywhere)
+    operands = [tables, orbitals, chosen, previous, inputs, parcel]
+    counts = [len(group) for group in operands]
+    counts += [len(orbitals), 2 if orbitals else 0, 1 if inputs else 0, len(parcel), len(fields), len(ring)]
+    operands = [array for group in operands for array in group]
+    return pl.pallas_call(
+        functools.partial(step_kernel, tuple(counts)),
+        out_shape=shapes,
+        in_specs=[vmem] * (len(operands) - len(parcel)) + [anywhere] * len(parcel),
+        out_specs=specs,
+        scratch_shapes=fields + ring,
         compiler_params=pltpu.CompilerParams(
-            collective_id=collective, has_side_effects=True, vmem_limit_bytes=48 * 1024 * 1024
+            collective_id=collective, has_side_effects=True, vmem_limit_bytes=56 * 1024 * 1024
         ),
-        cost_estimate=pl.CostEstimate(flops=0, bytes_accessed=20 * planes * points * 4, transcendentals=0),
-    )(*inputs, parcel)
+        cost_estimate=pl.CostEstimate(flops=flops, bytes_accessed=20 * planes * points * 4, transcendentals=0),
+    )(*operands)
 
 
 def whole_bands(orbitals, owner, picks):
@@ -395,12 +417,13 @@
         fetched.append(jnp.where(band == owner[step], rows, jnp.zeros_like(rows)))
     own = lax.dynamic_slice_in_dim(orbitals, slab * half, half, 0)
     sent = lax.dynamic_slice_in_dim(orbitals, (1 - slab) * half, half, 0)
-    chosen, other = ring_sum(fetched, sent, 1, 2, 0)
-    applied_own, applied_other, summed_own, summed_other = potentials((own, other), chosen)
-    summed = [part[step] for part in (summed_own, summed_other) for step in range(STEPS)]
-    transposed, back = ring_sum(summed, applied_other, 2, 1, 1)
-    exchange = jnp.where(slab == 0, jnp.concatenate([applied_own, back]), jnp.concatenate([back, applied_own]))
-    return exchange, transposed[0]
+    chosen, other = run_step(0, inputs=fetched[:1], parcel=[sent])
+    parts = [own, other]
+    *applied, summed_own, summed_other, chosen = run_step(1, parts, [chosen], inputs=fetched[1:])
+    *applied, late_own, late_other, early = run_step(2, parts, [chosen], applied, [summed_own, summed_other])
+    late, back = run_step(3, inputs=[late_own, late_other], parcel=applied[1:])
+    exchange = jnp.where(slab == 0, jnp.concatenate([applied[0], back]), jnp.concatenate([back, applied[0]]))
+    return exchange, jnp.concatenate([early, late])
 
 
 def broadcast(x, axis, root):

time: 296 us -> 338 us (1.14)
  Pallas kernels: 265 us -> 312 us
  local copies, waits for them, and re-layouts: 18.1 us -> 8.23 us
  other arithmetic: 2.35 us -> 8.42 us
    pallas_call x3 -> x4, Pallas kernels: 265 us -> 312 us  [run_step(): pl.pallas_call(functools.partial(step_kernel, tuple(counts)), out_shape=s...]
    unnamed x11 -> x8, local copies, waits for them, and re-layouts: 6.61 us -> 1.21 us
    squeeze x2 -> x0, local copies, waits for them, and re-layouts: 4.41 us -> none  [whole_bands(): part[step]]
where the time goes in v3:
time: 338 us
  Pallas kernels  312 us (92%)
  between operations  9.49 us (3%)
  other arithmetic  8.42 us (2%)
  local copies, waits for them, and re-layouts  8.23 us (2%)
    pallas_call x4, Pallas kernels, run_step(): pl.pallas_call(functools.partial(step_kernel, tuple(counts)), out_shape=s...  312 us

profile of v3, /device:TPU:0, one launch (start us, length us, event | category | flops | bytes accessed | tf_op | source)
XLA Modules:
  0.0 338.0 jit_solution(4122479244636179383)
XLA Ops:
  0.6 1.3 fusion.1
  3.3 1.4 fusion
  12.2 2.2 constant_dynamic-slice_fusion.1
  14.4 0.0 copy-start
  14.4 2.1 maximum_select_fusion.1
  16.5 1.2 copy-done
  17.7 2.1 constant_dynamic-slice_fusion.2
  19.7 77.2 %shard_map.140 = (f32[2,2,48,4608]{3,2,1,0:T(8,128)}, f32[2,48,4608]{2,1,0:T(8,128)}) custom-call(f32[2,48,4608]{2,1,0:T(8,128)} %get-tuple-element.42.refs_0_, f32[2,48,4608]{2,1,0:T(8,128)} %get-tuple-element.34.refs_1_), custom_call_target="tpu_custom_call" | custom-call | bytes 17694720 | tf_op jit(solution)/shard_map/pallas_call | solution.py:396
  96.9 78.9 %shard_map.141 = (f32[2,48,4608]{2,1,0:T(8,128)}, f32[2,48,4608]{2,1,0:T(8,128)}, f32[2,48,4608]{2,1,0:T(8,128)}, f32[2,48,4608]{2,1,0:T(8,128)}, f32[2,2,48,4608]{3,2,1,0:T(8,128)}) custom-call(bf16[2304,768]{1,0:T(8,128)(2,1)} %constant.38.clone.refs_0_, bf16[192,576]{1,0:T(8,128)(2,1)} %constant.39.clone.refs_1_, ...), custom_call_target="tpu_custom_call" | custom-call | flops 20384317440 | bytes 17694720 | tf_op jit(solution)/shard_map/pallas_call | solution.py:396
  175.8 84.8 %shard_map.142 = (f32[2,48,4608]{2,1,0:T(8,128)}, f32[2,48,4608]{2,1,0:T(8,128)}, f32[2,48,4608]{2,1,0:T(8,128)}, f32[2,48,4608]{2,1,0:T(8,128)}, f32[1,2,48,4608]{3,2,1,0:T(8,128)}) custom-call(bf16[2304,768]{1,0:T(8,128)(2,1)} %constant.38.clone.refs_0_, bf16[192,576]{1,0:T(8,128)(2,1)} %constant.39.clone.refs_1_, ...), custom_call_target="tpu_custom_call" | custom-call | flops 20384317440 | bytes 17694720 | tf_op jit(solution)/shard_map/pallas_call | solution.py:396
  260.6 0.0 copy-start.2
  260.6 70.9 %shard_map.143 = (f32[1,2,48,4608]{3,2,1,0:T(8,128)}, f32[2,48,4608]{2,1,0:T(8,128)}) custom-call(f32[2,48,4608]{2,1,0:T(8,128)} %get-tuple-element.24.refs_0_, f32[2,48,4608]{2,1,0:T(8,128)} %get-tuple-element.25.refs_1_, f32[2,48,4608]{2,1,0:T(8,128)} %get-tuple-element.26.refs_2_), custom_call_target="tpu_custom_call" | custom-call | bytes 17694720 | tf_op jit(solution)/shard_map/pallas_call | solution.py:396
  331.6 0.0 copy-done.2
  331.6 0.0 copy-start.1
  331.6 0.0 copy-start.3
  331.6 4.3 %maximum_select_fusion = f32[4,48,4608]{2,1,0:T(8,128)} fusion(f32[2,48,4608]{2,1,0:T(8,128)} %get-tuple-element.27, f32[2,48,4608]{2,1,0:T(8,128)S(1)} %copy-done.2, pred[]{:T(512)S(6)} %eq.9), kind=kLoop, calls=%fused_computation | loop fusion | flops 2654208 | bytes 7077889 | tf_op jit(solution)/shard_map/jit(_where)/select_n | solution.py:425
  335.9 0.0 copy-done.1
  335.9 0.0 copy-done.3
  335.9 2.1 pad_maximum_fusion
Async XLA Ops:
  14.4 3.3 copy-start
  260.6 71.0 %copy-start.2 = (f32[2,48,4608]{2,1,0:T(8,128)S(1)}, f32[2,48,4608]{2,1,0:T(8,128)}, u32[]{:S(2)}) copy-start(f32[2,48,4608]{2,1,0:T(8,128)} %get-tuple-element.23) | copy-start | bytes 5308420
  331.6 4.3 %copy-start.1 = (f32[1,2,48,4608]{3,2,1,0:T(8,128)S(1)}, f32[1,2,48,4608]{3,2,1,0:T(8,128)}, u32[]{:S(2)}) copy-start(f32[1,2,48,4608]{3,2,1,0:T(8,128)} %get-tuple-element.28) | copy-start | bytes 5308420
  331.6 4.3 %copy-start.3 = (f32[1,2,48,4608]{3,2,1,0:T(8,128)S(1)}, f32[1,2,48,4608]{3,2,1,0:T(8,128)}, u32[]{:S(2)}) copy-start(f32[1,2,48,4608]{3,2,1,0:T(8,128)} %get-tuple-element.29) | copy-start | bytes 5308420

commit v4 on v2

--- a/solution.py
+++ b/solution.py
@@ -286,7 +286,7 @@
         lanes = pl.ds(pl.multiple_of((chunk % BLOCKS) * width, 128), width)
         return chunk // BLOCKS, pl.ds(way * half, half), lanes
 
-    parcel = push(parcel_ref, got_ref, lone_send.at[0], lone_recv.at[0], across)
+    parcels = [push(parcel_ref.at[0], got_ref.at[0], lone_send.at[0], lone_recv.at[0], across)]
 
     swaps = []
     for at, ref in enumerate(inputs):
@@ -318,11 +318,13 @@
             cross_ref[0, rows, :] = done[1]
     if slabs_in == 2:
         crossing = push(cross_ref.at[0], cross_ref.at[1], lone_send.at[1], lone_recv.at[1], across)
+        parcels.append(push(parcel_ref.at[1], got_ref.at[1], lone_send.at[2], lone_recv.at[2], across))
         crossing.wait_recv()
         out_ref[0, step, core, :, lanes] += cross_ref[1]
     else:
         own = out_ref.at[0, step, core, :, lanes]
         crossing = push(own, out_ref.at[1, step, core, :, lanes], lone_send.at[1], lone_recv.at[1], across)
+        parcels.append(push(parcel_ref.at[1], got_ref.at[1], lone_send.at[2], lone_recv.at[2], across))
 
     hands = []
     last = {}
@@ -346,7 +348,8 @@
     crossing.wait_send()
     for copy in hands:
         copy.wait()
-    parcel.wait()
+    for copy in parcels:
+        copy.wait()
 
 
 def ring_sum(inputs, parcel, slabs_in, slabs_out, collective):
@@ -370,8 +373,8 @@
             dma((len(inputs),)),
             dma((2, RING - 1)),
             dma((2, RING - 1)),
-            dma((2,)),
-            dma((2,)),
+            dma((3,)),
+            dma((3,)),
             dma((slabs_out, 2, RING - 1)),
             dma((slabs_out, 2, RING - 1)),
             dma((slabs_out, 2, RING)),

time: 296 us -> 294 us (level)
  no operation moved by 1% of the time
where the time goes in v4:
time: 294 us
  Pallas kernels  264 us (90%)
  local copies, waits for them, and re-layouts  18.1 us (6%)
  between operations  9.65 us (3%)
    pallas_call x2, Pallas kernels, ring_sum(): pl.pallas_call(functools.partial(ring_kernel, slabs_in, slabs_out), out_s...  173 us
    pallas_call x1, Pallas kernels, potentials(): pl.pallas_call(potential_kernel, grid=(count, STEPS), out_shape=[band_sha...  90.7 us
    unnamed x11, local copies, waits for them, and re-layouts  6.61 us

profile of v4, /device:TPU:0, one launch (start us, length us, event | category | flops | bytes accessed | tf_op | source)
XLA Modules:
  0.0 293.6 jit_solution(15671129220989638080)
XLA Ops:
  0.6 1.3 fusion.1
  3.3 1.5 fusion
  12.4 2.2 constant_dynamic-slice_fusion.2
  14.6 0.0 copy-start.1
  14.6 0.3 maximum_select_fusion.1
  14.9 1.7 copy-done.1
  16.6 2.1 constant_dynamic-slice_fusion
  18.6 81.7 %shard_map.95 = (f32[2,2,2,48,4608]{4,3,2,1,0:T(8,128)}, f32[2,48,4608]{2,1,0:T(8,128)S(1)}) custom-call(f32[2,48,4608]{2,1,0:T(8,128)S(1)} %get-tuple-element.34.refs_0_, f32[2,48,4608]{2,1,0:T(8,128)S(1)} %get-tuple-element.35.refs_1_, f32[2,48,4608]{2,1,0:T(8,128)} %get-tuple-element.22.refs_2_), custom_call_target="tpu_custom_call" | custom-call | bytes 17694720 | tf_op jit(solution)/shard_map/pallas_call | solution.py:362
  100.3 0.0 copy-start
  100.3 1.2 copy-done
  101.6 90.7 %shard_map.96 = (f32[2,48,4608]{2,1,0:T(8,128)}, f32[2,48,4608]{2,1,0:T(8,128)}, f32[2,2,48,4608]{3,2,1,0:T(8,128)}, f32[2,2,48,4608]{3,2,1,0:T(8,128)}) custom-call(bf16[2304,768]{1,0:T(8,128)(2,1)} %constant.38.clone.refs_0_, bf16[192,576]{1,0:T(8,128)(2,1)} %constant.39.clone.refs_1_, bf16[192,576]{1,0:T(8,128)(2,1)} %constant.40.clone.refs_2_, ...), custom_call_target="tpu_custom_call" | custom-call | flops 40768634880 | bytes 28311552 | tf_op jit(solution)/shard_map/pallas_call | solution.py:223
  192.3 0.0 copy-start.2
  192.3 2.4 slice_bitcast_fusion.2
  194.7 0.7 copy-done.2
  195.4 2.0 slice_bitcast_fusion
  197.4 0.0 copy-start.4
  197.4 91.1 %shard_map.97 = (f32[1,2,2,48,4608]{4,3,2,1,0:T(8,128)}, f32[2,48,4608]{2,1,0:T(8,128)S(1)}) custom-call(f32[2,48,4608]{2,1,0:T(8,128)S(1)} %get-tuple-element.21.refs_0_, f32[2,48,4608]{2,1,0:T(8,128)S(1)} %get-tuple-element.20.refs_1_, f32[2,48,4608]{2,1,0:T(8,128)} %get-tuple-element.19.refs_2_, f32[2,48,4608]{2,1,0:T(8,128)} %get-tuple-element.18.refs_3_, ...), custom_call_target="tpu_custom_call" | custom-call | bytes 17694720 | tf_op jit(solution)/shard_map/pallas_call | solution.py:362
  288.5 0.0 copy-done.4
  288.5 0.0 copy-start.3
  288.5 2.1 maximum_select_fusion
  290.6 1.2 copy-done.3
  291.8 1.8 copy.11
Async XLA Ops:
  14.6 2.0 copy-start.1
  100.3 1.2 copy-start
  192.3 3.1 %copy-start.2 = (f32[2,2,48,4608]{3,2,1,0:T(8,128)S(1)}, f32[2,2,48,4608]{3,2,1,0:T(8,128)}, u32[]{:S(2)}) copy-start(f32[2,2,48,4608]{3,2,1,0:T(8,128)} %get-tuple-element.14) | copy-start | bytes 10616836
  197.4 91.1 %copy-start.4 = (f32[2,48,4608]{2,1,0:T(8,128)S(1)}, f32[2,48,4608]{2,1,0:T(8,128)}, u32[]{:S(2)}) copy-start(f32[2,48,4608]{2,1,0:T(8,128)} %get-tuple-element.12) | copy-start | bytes 5308420
  288.5 3.3 %copy-start.3 = (f32[1,2,2,48,4608]{4,3,2,1,0:T(8,128)S(1)}, f32[1,2,2,48,4608]{4,3,2,1,0:T(8,128)}, u32[]{:S(2)}) copy-start(f32[1,2,2,48,4608]{4,3,2,1,0:T(8,128)} %get-tuple-element.17) | copy-start | bytes 10616836
